TPU v7x, 256 devices: a whole 4x4x8 slice. The times are simulated.
256 devices in a mesh: gx: 16 (over z_lo, y), gy: 16 (over x, z_hi, core).
Axes of the slice: x: 4, y: 4, z: 8 (z_hi: 2, z_lo: 4; z = z_hi * 4 + z_lo), core: 2. Of those that a mesh axis runs over, the one named last changes fastest.
Arguments:
- electric: float32 [3, 32, 512, 2048], P(None, None, 'gx', 'gy'), may hold values from -6 to 6
- magnetic: float32 [3, 32, 512, 2048], P(None, None, 'gx', 'gy'), may hold values from -6 to 6
- forward_field: float32 [3, 32, 512, 2048], P(None, None, 'gx', 'gy'), may hold values from -6 to 6
- material: int32 [32, 512, 2048], P(None, 'gx', 'gy'), may hold values from 0 to 3
- inv_permittivity: float32 [4], replicated, may hold values from 0.08 to 1
- spectral_rate: float32 [128], replicated, may hold values from 0.2 to 1.2
- intersection_partial: float32 [32, 512, 128], P('gx', 'gy'), may hold values from -0.3125 to 0.3125
- mode_profile: float32 [32, 32, 16384], P('gy', None, 'gx'), may hold values from -1 to 1
- sheet_offset: int32 [16], P('gy'), may hold values from 2 to 125
- plane_start: int32 [16], P('gy'), may hold values from 0 to 255
- monitor_length: int32 [16], P('gy'), may hold values from 128 to 256
Outputs:
- electric_out: float32 [3, 32, 512, 2048], P(None, None, 'gx', 'gy')
- magnetic_out: float32 [3, 32, 512, 2048], P(None, None, 'gx', 'gy')
- gradient: float32 [32, 512, 2048], P(None, 'gx', 'gy')
All inputs are finite; a program needn't handle non-finite values.
Results may differ from a plain program's by a relative error of at most 0.0003.
Values sent between devices are 32-bit elements; how exact they have to be, the bound alone decides.
A program may use at most 192 MiB of HBM per device.

v0:
```python
import jax
import jax.numpy as jnp
from jax import lax
from jax.sharding import PartitionSpec as P

SPAN_TICKS = 16


COURANT = 0.5


def shifted(block, axis, distance):
    devices = range(lax.axis_size(axis))
    route = [(i - distance, i) for i in devices if i - distance in devices]
    return lax.ppermute(block, axis, route)


def ahead(field, ghost, along_axis):
    size = field.shape[along_axis]
    rest = lax.slice_in_dim(field, 1, size, axis=along_axis)
    return jnp.concatenate([rest, ghost], axis=along_axis)


def behind(field, ghost, along_axis):
    size = field.shape[along_axis]
    rest = lax.slice_in_dim(field, 0, size - 1, axis=along_axis)
    return jnp.concatenate([ghost, rest], axis=along_axis)


def update_magnetic(electric, magnetic, ghost_x, ghost_y):
    electric_x, electric_field_y, electric_z = electric
    zeros_zface = jnp.zeros_like(electric_x[:1])
    magnetic_x = magnetic[0] - COURANT * (
        ahead(electric_z, ghost_y[1], 2)
        - electric_z
        - (ahead(electric_field_y, zeros_zface, 0) - electric_field_y)
    )
    magnetic_y = magnetic[1] - COURANT * (
        ahead(electric_x, zeros_zface, 0)
        - electric_x
        - (ahead(electric_z, ghost_x[1], 1) - electric_z)
    )
    magnetic_z = magnetic[2] - COURANT * (
        ahead(electric_field_y, ghost_x[0], 1)
        - electric_field_y
        - (ahead(electric_x, ghost_y[0], 2) - electric_x)
    )
    return (magnetic_x, magnetic_y, magnetic_z)


def advance_displacement(electric, magnetic, coupling, ghost_x, ghost_y):
    magnetic_x, magnetic_y, magnetic_z = magnetic
    zeros_zface = jnp.zeros_like(magnetic_x[:1])
    electric_x = electric[0] + coupling * (
        magnetic_z
        - behind(magnetic_z, ghost_y[1], 2)
        - (magnetic_y - behind(magnetic_y, zeros_zface, 0))
    )
    electric_field_y = electric[1] + coupling * (
        magnetic_x
        - behind(magnetic_x, zeros_zface, 0)
        - (magnetic_z - behind(magnetic_z, ghost_x[1], 1))
    )
    electric_z = electric[2] + coupling * (
        magnetic_y
        - behind(magnetic_y, ghost_x[0], 1)
        - (magnetic_x - behind(magnetic_x, ghost_y[0], 2))
    )
    return (electric_x, electric_field_y, electric_z)


def inject(electric, current, moment, column):
    current_now = lax.dynamic_index_in_dim(current, moment, 1, keepdims=False)
    width_y = electric[0].shape[2]
    sheet_row = (jnp.arange(width_y, dtype=jnp.int32) == column).astype(jnp.float32)
    electric_x = electric[0] + current_now[0][..., None] * sheet_row
    electric_z = electric[2] + current_now[1][..., None] * sheet_row
    return (electric_x, electric[1], electric_z)


def synthesize(profile, coefficients, cells_x, first_cell, final_cell):
    extent_mask = ((cells_x >= first_cell) & (cells_x < final_cell)).astype(jnp.float32)
    current = jnp.einsum("mt,cmxz->ctzx", coefficients, profile, precision=lax.Precision.HIGHEST)
    return current * extent_mask


def accumulate(total, electric, forward_field):
    return total + (
        electric[0] * forward_field[0]
        + electric[1] * forward_field[1]
        + electric[2] * forward_field[2]
    )


def shards(
    electric,
    magnetic,
    forward_field,
    material,
    inv_permittivity,
    spectral_rate,
    intersection_partial,
    mode_profile,
    sheet_offset,
    plane_start,
    monitor_length,
):
    highest = lax.Precision.HIGHEST
    slab_depth, width_x, width_y = (electric.shape[1], electric.shape[2], electric.shape[3])
    mode_count = mode_profile.shape[1]
    label_count = inv_permittivity.shape[0]
    label_match = (
        material[None] == jnp.arange(label_count, dtype=jnp.int32)[:, None, None, None]
    ).astype(jnp.float32)
    coupling = COURANT * jnp.sum(label_match * inv_permittivity[:, None, None, None], axis=0)
    tick_moments = jnp.arange(SPAN_TICKS).astype(jnp.float32)
    rotation_radians = spectral_rate[:, None] * tick_moments[None, :]
    cosine_table = jnp.cos(rotation_radians)
    sine_table = jnp.sin(rotation_radians)
    cotangent = lax.psum(intersection_partial, "gx")
    coefficients = jnp.dot(cotangent[0], cosine_table, precision=highest) - jnp.dot(
        cotangent[1], sine_table, precision=highest
    )
    first_cell = plane_start[0]
    final_cell = plane_start[0] + monitor_length[0]
    column = sheet_offset[0]
    anchor_x = lax.axis_index("gx") * width_x
    profile = mode_profile.reshape(2, mode_count, width_x, slab_depth)
    gradient = jnp.zeros((slab_depth, width_x, width_y), jnp.float32)
    fields_e = (electric[0], electric[1], electric[2])
    fields_h = (magnetic[0], magnetic[1], magnetic[2])
    cells_x = anchor_x + jnp.arange(width_x, dtype=jnp.int32)
    current = synthesize(profile, coefficients, cells_x, first_cell, final_cell)

    def one_step(moment, carried):
        field_e, curl_partner, total = carried
        xface_e = jnp.stack([field_e[1][:, 0, :], field_e[2][:, 0, :]])
        ghost_x = shifted(xface_e, "gx", -1)[:, :, None, :]
        yface_e = jnp.stack([field_e[0][:, :, 0], field_e[2][:, :, 0]]).reshape(
            2, slab_depth * width_x
        )
        ghost_y = shifted(yface_e, "gy", -1).reshape(2, slab_depth, width_x, 1)
        curl_partner = update_magnetic(field_e, curl_partner, ghost_x, ghost_y)
        xface_h = jnp.stack([curl_partner[1][:, -1, :], curl_partner[2][:, -1, :]])
        lower_x = shifted(xface_h, "gx", 1)[:, :, None, :]
        yface_h = jnp.stack([curl_partner[0][:, :, -1], curl_partner[2][:, :, -1]]).reshape(
            2, slab_depth * width_x
        )
        lower_y = shifted(yface_h, "gy", 1).reshape(2, slab_depth, width_x, 1)
        field_e = advance_displacement(field_e, curl_partner, coupling, lower_x, lower_y)
        field_e = inject(field_e, current, moment, column)
        total = accumulate(total, field_e, forward_field)
        return (field_e, curl_partner, total)

    fields_e, fields_h, gradient = lax.fori_loop(
        0, SPAN_TICKS, one_step, (fields_e, fields_h, gradient)
    )
    return (jnp.stack(fields_e), jnp.stack(fields_h), gradient / SPAN_TICKS)


def solution(mesh):
    placed = (
        P(None, None, "gx", "gy"),
        P(None, None, "gx", "gy"),
        P(None, None, "gx", "gy"),
        P(None, "gx", "gy"),
        P(),
        P(),
        P("gx", "gy", None),
        P("gy", None, "gx"),
        P("gy"),
        P("gy"),
        P("gy"),
    )
    return jax.shard_map(
        shards,
        mesh=mesh,
        in_specs=placed,
        out_specs=(P(None, None, "gx", "gy"), P(None, None, "gx", "gy"), P(None, "gx", "gy")),
        check_vma=False,
    )
```

profile of v0, /device:TPU:33, one launch (start us, length us, event | category | flops | bytes accessed | tf_op | source)
XLA Modules:
  0.0 795.9 jit_solution(5908969977341990262)
XLA Ops:
  0.6 59.6 %psum.7 = f32[2,32,128]{2,1,0:T(8,128)S(1)} all-reduce(f32[2,32,128]{2,1,0:T(8,128)} %param.19), channel_id=1, replica_groups=mesh['gx'=16,'gy'=16] {'gx'}, use_global_device_ids=true, to_apply=%region_1.0 | all-reduce | flops 8192 | bytes 65536 | tf_op jit(solution)/shard_map/psum | solution.py:120
  74.5 715.8 %while.26 = (s32[]{:T(128)}, f32[32,32,128]{2,0,1:T(8,128)S(1)}, f32[32,32,128]{2,0,1:T(8,128)S(1)}, f32[32,32,128]{2,0,1:T(8,128)S(1)}, f32[32,32,128]{2,0,1:T(...) while((s32[]{:T(128)}, f32[32,32,128]{2,0,1:T(8,128)S(1)}, ...), condition=%wide.region_3.4_spmd.clone, body=%wide.region_2.3_spmd.clone.sunk | while | flops 6443267 | bytes 27960628 | solution.py:155
  77.4 16.6 %collective-permute-start.1 = (f32[2,1024]{1,0:T(2,128)S(1)}, f32[2,1024]{1,0:T(2,128)S(1)}, u32[]{:S(2)}, u32[]{:S(2)}) collective-permute-start(f32[2,1024]{1,0:T(2,128)S(1)} %pad_maximum_fusion.11), channel_id=1, source_target_pairs={{1,0},{2,1},{3,2},{4,3},{5,4},{6,5},{7,6},{8,7},{9,8},{10,9},{11,1... | collective-permute-start | bytes 24584 | tf_op jit(solution)/shard_map/while/body/eval_jaxpr/ppermute | solution.py:15
  111.7 6.0 collective-permute-start.2
  155.7 7.5 collective-permute-start.2
  172.0 3.7 fusion.40
  199.6 7.5 collective-permute-start.2
  243.2 7.5 collective-permute-start.2
  286.8 7.5 collective-permute-start.2
  330.4 7.5 collective-permute-start.2
  346.4 3.7 fusion.40
  374.0 7.5 collective-permute-start.2
  417.6 7.5 collective-permute-start.2
  461.2 7.5 collective-permute-start.2
  477.2 3.7 fusion.40
  504.8 7.5 collective-permute-start.2
  520.8 3.7 fusion.40
  548.4 7.5 collective-permute-start.2
  592.6 7.6 collective-permute-start.2
  637.1 7.6 collective-permute-start.2
  681.6 7.6 collective-permute-start.2
  697.6 3.7 fusion.40
  726.1 7.6 collective-permute-start.2
  770.6 7.6 collective-permute-start.2
  (815 shorter events, 577.3 us)
Async XLA Ops:
  74.6 29.2 %collective-permute-start = (f32[2,32,128]{2,1,0:T(8,128)S(1)}, f32[2,32,128]{2,1,0:T(8,128)S(1)}, u32[]{:S(2)}, u32[]{:S(2)}) collective-permute-start(f32[2,32,128]{2,1,0:T(8,128)S(1)} %pad_maximum_fusion.10), channel_id=1, source_target_pairs={{16,0},{32,16},{48,32},{64,48},{80,64},{96,80},{112,96},{128,112},... | collective-permute-start | bytes 98312 | tf_op jit(solution)/shard_map/while/body/eval_jaxpr/ppermute | solution.py:15
  77.4 23.6 %collective-permute-start.1 = (f32[2,1024]{1,0:T(2,128)S(1)}, f32[2,1024]{1,0:T(2,128)S(1)}, u32[]{:S(2)}, u32[]{:S(2)}) collective-permute-start(f32[2,1024]{1,0:T(2,128)S(1)} %pad_maximum_fusion.11), channel_id=1, source_target_pairs={{1,0},{2,1},{3,2},{4,3},{5,4},{6,5},{7,6},{8,7},{9,8},{10,9},{11,1... | collective-permute-start | bytes 24584 | tf_op jit(solution)/shard_map/while/body/eval_jaxpr/ppermute | solution.py:15
  111.7 11.3 %collective-permute-start.2 = (f32[2,1024]{1,0:T(2,128)S(1)}, f32[2,1024]{1,0:T(2,128)S(1)}, u32[]{:S(2)}, u32[]{:S(2)}) collective-permute-start(f32[2,1024]{1,0:T(2,128)S(1)} %pad_maximum_fusion.12), channel_id=1, source_target_pairs={{0,1},{1,2},{2,3},{3,4},{4,5},{5,6},{6,7},{7,8},{8,9},{9,10},{10,1... | collective-permute-start | bytes 24584 | tf_op jit(solution)/shard_map/while/body/eval_jaxpr/ppermute | solution.py:15
  131.8 16.0 %collective-permute-start = (f32[2,32,128]{2,1,0:T(8,128)S(1)}, f32[2,32,128]{2,1,0:T(8,128)S(1)}, u32[]{:S(2)}, u32[]{:S(2)}) collective-permute-start(f32[2,32,128]{2,1,0:T(8,128)S(1)} %pad_maximum_fusion.10), channel_id=1, source_target_pairs={{16,0},{32,16},{48,32},{64,48},{80,64},{96,80},{112,96},{128,112},... | collective-permute-start | bytes 98312 | tf_op jit(solution)/shard_map/while/body/eval_jaxpr/ppermute | solution.py:15
  175.7 16.0 %collective-permute-start = (f32[2,32,128]{2,1,0:T(8,128)S(1)}, f32[2,32,128]{2,1,0:T(8,128)S(1)}, u32[]{:S(2)}, u32[]{:S(2)}) collective-permute-start(f32[2,32,128]{2,1,0:T(8,128)S(1)} %pad_maximum_fusion.10), channel_id=1, source_target_pairs={{16,0},{32,16},{48,32},{64,48},{80,64},{96,80},{112,96},{128,112},... | collective-permute-start | bytes 98312 | tf_op jit(solution)/shard_map/while/body/eval_jaxpr/ppermute | solution.py:15
  219.3 16.0 %collective-permute-start = (f32[2,32,128]{2,1,0:T(8,128)S(1)}, f32[2,32,128]{2,1,0:T(8,128)S(1)}, u32[]{:S(2)}, u32[]{:S(2)}) collective-permute-start(f32[2,32,128]{2,1,0:T(8,128)S(1)} %pad_maximum_fusion.10), channel_id=1, source_target_pairs={{16,0},{32,16},{48,32},{64,48},{80,64},{96,80},{112,96},{128,112},... | collective-permute-start | bytes 98312 | tf_op jit(solution)/shard_map/while/body/eval_jaxpr/ppermute | solution.py:15
  262.9 16.0 %collective-permute-start = (f32[2,32,128]{2,1,0:T(8,128)S(1)}, f32[2,32,128]{2,1,0:T(8,128)S(1)}, u32[]{:S(2)}, u32[]{:S(2)}) collective-permute-start(f32[2,32,128]{2,1,0:T(8,128)S(1)} %pad_maximum_fusion.10), channel_id=1, source_target_pairs={{16,0},{32,16},{48,32},{64,48},{80,64},{96,80},{112,96},{128,112},... | collective-permute-start | bytes 98312 | tf_op jit(solution)/shard_map/while/body/eval_jaxpr/ppermute | solution.py:15
  306.5 16.0 %collective-permute-start = (f32[2,32,128]{2,1,0:T(8,128)S(1)}, f32[2,32,128]{2,1,0:T(8,128)S(1)}, u32[]{:S(2)}, u32[]{:S(2)}) collective-permute-start(f32[2,32,128]{2,1,0:T(8,128)S(1)} %pad_maximum_fusion.10), channel_id=1, source_target_pairs={{16,0},{32,16},{48,32},{64,48},{80,64},{96,80},{112,96},{128,112},... | collective-permute-start | bytes 98312 | tf_op jit(solution)/shard_map/while/body/eval_jaxpr/ppermute | solution.py:15
  350.1 16.0 %collective-permute-start = (f32[2,32,128]{2,1,0:T(8,128)S(1)}, f32[2,32,128]{2,1,0:T(8,128)S(1)}, u32[]{:S(2)}, u32[]{:S(2)}) collective-permute-start(f32[2,32,128]{2,1,0:T(8,128)S(1)} %pad_maximum_fusion.10), channel_id=1, source_target_pairs={{16,0},{32,16},{48,32},{64,48},{80,64},{96,80},{112,96},{128,112},... | collective-permute-start | bytes 98312 | tf_op jit(solution)/shard_map/while/body/eval_jaxpr/ppermute | solution.py:15
  393.7 16.0 %collective-permute-start = (f32[2,32,128]{2,1,0:T(8,128)S(1)}, f32[2,32,128]{2,1,0:T(8,128)S(1)}, u32[]{:S(2)}, u32[]{:S(2)}) collective-permute-start(f32[2,32,128]{2,1,0:T(8,128)S(1)} %pad_maximum_fusion.10), channel_id=1, source_target_pairs={{16,0},{32,16},{48,32},{64,48},{80,64},{96,80},{112,96},{128,112},... | collective-permute-start | bytes 98312 | tf_op jit(solution)/shard_map/while/body/eval_jaxpr/ppermute | solution.py:15
  437.3 16.0 %collective-permute-start = (f32[2,32,128]{2,1,0:T(8,128)S(1)}, f32[2,32,128]{2,1,0:T(8,128)S(1)}, u32[]{:S(2)}, u32[]{:S(2)}) collective-permute-start(f32[2,32,128]{2,1,0:T(8,128)S(1)} %pad_maximum_fusion.10), channel_id=1, source_target_pairs={{16,0},{32,16},{48,32},{64,48},{80,64},{96,80},{112,96},{128,112},... | collective-permute-start | bytes 98312 | tf_op jit(solution)/shard_map/while/body/eval_jaxpr/ppermute | solution.py:15
  480.9 16.0 %collective-permute-start = (f32[2,32,128]{2,1,0:T(8,128)S(1)}, f32[2,32,128]{2,1,0:T(8,128)S(1)}, u32[]{:S(2)}, u32[]{:S(2)}) collective-permute-start(f32[2,32,128]{2,1,0:T(8,128)S(1)} %pad_maximum_fusion.10), channel_id=1, source_target_pairs={{16,0},{32,16},{48,32},{64,48},{80,64},{96,80},{112,96},{128,112},... | collective-permute-start | bytes 98312 | tf_op jit(solution)/shard_map/while/body/eval_jaxpr/ppermute | solution.py:15
  524.5 16.0 %collective-permute-start = (f32[2,32,128]{2,1,0:T(8,128)S(1)}, f32[2,32,128]{2,1,0:T(8,128)S(1)}, u32[]{:S(2)}, u32[]{:S(2)}) collective-permute-start(f32[2,32,128]{2,1,0:T(8,128)S(1)} %pad_maximum_fusion.10), channel_id=1, source_target_pairs={{16,0},{32,16},{48,32},{64,48},{80,64},{96,80},{112,96},{128,112},... | collective-permute-start | bytes 98312 | tf_op jit(solution)/shard_map/while/body/eval_jaxpr/ppermute | solution.py:15
  548.4 11.7 %collective-permute-start.2 = (f32[2,1024]{1,0:T(2,128)S(1)}, f32[2,1024]{1,0:T(2,128)S(1)}, u32[]{:S(2)}, u32[]{:S(2)}) collective-permute-start(f32[2,1024]{1,0:T(2,128)S(1)} %pad_maximum_fusion.12), channel_id=1, source_target_pairs={{0,1},{1,2},{2,3},{3,4},{4,5},{5,6},{6,7},{7,8},{8,9},{9,10},{10,1... | collective-permute-start | bytes 24584 | tf_op jit(solution)/shard_map/while/body/eval_jaxpr/ppermute | solution.py:15
  568.1 16.5 %collective-permute-start = (f32[2,32,128]{2,1,0:T(8,128)S(1)}, f32[2,32,128]{2,1,0:T(8,128)S(1)}, u32[]{:S(2)}, u32[]{:S(2)}) collective-permute-start(f32[2,32,128]{2,1,0:T(8,128)S(1)} %pad_maximum_fusion.10), channel_id=1, source_target_pairs={{16,0},{32,16},{48,32},{64,48},{80,64},{96,80},{112,96},{128,112},... | collective-permute-start | bytes 98312 | tf_op jit(solution)/shard_map/while/body/eval_jaxpr/ppermute | solution.py:15
  592.6 12.1 %collective-permute-start.2 = (f32[2,1024]{1,0:T(2,128)S(1)}, f32[2,1024]{1,0:T(2,128)S(1)}, u32[]{:S(2)}, u32[]{:S(2)}) collective-permute-start(f32[2,1024]{1,0:T(2,128)S(1)} %pad_maximum_fusion.12), channel_id=1, source_target_pairs={{0,1},{1,2},{2,3},{3,4},{4,5},{5,6},{6,7},{7,8},{8,9},{9,10},{10,1... | collective-permute-start | bytes 24584 | tf_op jit(solution)/shard_map/while/body/eval_jaxpr/ppermute | solution.py:15
  612.4 16.8 %collective-permute-start = (f32[2,32,128]{2,1,0:T(8,128)S(1)}, f32[2,32,128]{2,1,0:T(8,128)S(1)}, u32[]{:S(2)}, u32[]{:S(2)}) collective-permute-start(f32[2,32,128]{2,1,0:T(8,128)S(1)} %pad_maximum_fusion.10), channel_id=1, source_target_pairs={{16,0},{32,16},{48,32},{64,48},{80,64},{96,80},{112,96},{128,112},... | collective-permute-start | bytes 98312 | tf_op jit(solution)/shard_map/while/body/eval_jaxpr/ppermute | solution.py:15
  637.1 12.1 %collective-permute-start.2 = (f32[2,1024]{1,0:T(2,128)S(1)}, f32[2,1024]{1,0:T(2,128)S(1)}, u32[]{:S(2)}, u32[]{:S(2)}) collective-permute-start(f32[2,1024]{1,0:T(2,128)S(1)} %pad_maximum_fusion.12), channel_id=1, source_target_pairs={{0,1},{1,2},{2,3},{3,4},{4,5},{5,6},{6,7},{7,8},{8,9},{9,10},{10,1... | collective-permute-start | bytes 24584 | tf_op jit(solution)/shard_map/while/body/eval_jaxpr/ppermute | solution.py:15
  656.9 16.8 %collective-permute-start = (f32[2,32,128]{2,1,0:T(8,128)S(1)}, f32[2,32,128]{2,1,0:T(8,128)S(1)}, u32[]{:S(2)}, u32[]{:S(2)}) collective-permute-start(f32[2,32,128]{2,1,0:T(8,128)S(1)} %pad_maximum_fusion.10), channel_id=1, source_target_pairs={{16,0},{32,16},{48,32},{64,48},{80,64},{96,80},{112,96},{128,112},... | collective-permute-start | bytes 98312 | tf_op jit(solution)/shard_map/while/body/eval_jaxpr/ppermute | solution.py:15
  681.6 12.1 %collective-permute-start.2 = (f32[2,1024]{1,0:T(2,128)S(1)}, f32[2,1024]{1,0:T(2,128)S(1)}, u32[]{:S(2)}, u32[]{:S(2)}) collective-permute-start(f32[2,1024]{1,0:T(2,128)S(1)} %pad_maximum_fusion.12), channel_id=1, source_target_pairs={{0,1},{1,2},{2,3},{3,4},{4,5},{5,6},{6,7},{7,8},{8,9},{9,10},{10,1... | collective-permute-start | bytes 24584 | tf_op jit(solution)/shard_map/while/body/eval_jaxpr/ppermute | solution.py:15
  701.4 16.8 %collective-permute-start = (f32[2,32,128]{2,1,0:T(8,128)S(1)}, f32[2,32,128]{2,1,0:T(8,128)S(1)}, u32[]{:S(2)}, u32[]{:S(2)}) collective-permute-start(f32[2,32,128]{2,1,0:T(8,128)S(1)} %pad_maximum_fusion.10), channel_id=1, source_target_pairs={{16,0},{32,16},{48,32},{64,48},{80,64},{96,80},{112,96},{128,112},... | collective-permute-start | bytes 98312 | tf_op jit(solution)/shard_map/while/body/eval_jaxpr/ppermute | solution.py:15
  726.1 12.1 %collective-permute-start.2 = (f32[2,1024]{1,0:T(2,128)S(1)}, f32[2,1024]{1,0:T(2,128)S(1)}, u32[]{:S(2)}, u32[]{:S(2)}) collective-permute-start(f32[2,1024]{1,0:T(2,128)S(1)} %pad_maximum_fusion.12), channel_id=1, source_target_pairs={{0,1},{1,2},{2,3},{3,4},{4,5},{5,6},{6,7},{7,8},{8,9},{9,10},{10,1... | collective-permute-start | bytes 24584 | tf_op jit(solution)/shard_map/while/body/eval_jaxpr/ppermute | solution.py:15
  745.9 16.8 %collective-permute-start = (f32[2,32,128]{2,1,0:T(8,128)S(1)}, f32[2,32,128]{2,1,0:T(8,128)S(1)}, u32[]{:S(2)}, u32[]{:S(2)}) collective-permute-start(f32[2,32,128]{2,1,0:T(8,128)S(1)} %pad_maximum_fusion.10), channel_id=1, source_target_pairs={{16,0},{32,16},{48,32},{64,48},{80,64},{96,80},{112,96},{128,112},... | collective-permute-start | bytes 98312 | tf_op jit(solution)/shard_map/while/body/eval_jaxpr/ppermute | solution.py:15
  770.6 12.1 %collective-permute-start.2 = (f32[2,1024]{1,0:T(2,128)S(1)}, f32[2,1024]{1,0:T(2,128)S(1)}, u32[]{:S(2)}, u32[]{:S(2)}) collective-permute-start(f32[2,1024]{1,0:T(2,128)S(1)} %pad_maximum_fusion.12), channel_id=1, source_target_pairs={{0,1},{1,2},{2,3},{3,4},{4,5},{5,6},{6,7},{7,8},{8,9},{9,10},{10,1... | collective-permute-start | bytes 24584 | tf_op jit(solution)/shard_map/while/body/eval_jaxpr/ppermute | solution.py:15
  (46 other events, 421.9 us)
where the time goes:
time: 807 us; the launch traced here: 796 us
  local copies, waits for them, and re-layouts  317 us (39%)
  starting transfers between devices  255 us (32%)
  other arithmetic  122 us (15%)
  blocking collectives  59.6 us (7%)
  waiting for transfers between devices  33.5 us (4%)
    ppermute x64, starting transfers between devices, shifted(): return lax.ppermute(block, axis, route)  255 us
    slice x96, local copies, waits for them, and re-layouts, ahead(): rest = lax.slice_in_dim(field, 1, size, axis=along_axis)  86.1 us
    psum x1, blocking collectives, shards(): cotangent = lax.psum(intersection_partial, 'gx')  59.6 us
    add x16, other arithmetic, accumulate(): total + (electric[0] * forward_field[0] + electric[1] * forward_field[1]...  59.2 us
    sub x16, other arithmetic, update_magnetic(): magnetic[1]  48.1 us
    slice x32, local copies, waits for them, and re-layouts, one_step(): curl_partner[0][:, :, -1]  37.7 us
    slice x32, local copies, waits for them, and re-layouts, one_step(): curl_partner[2][:, :, -1]  37.7 us
    ppermute x64, waiting for transfers between devices, shifted(): return lax.ppermute(block, axis, route)  33.5 us
  transfers between devices with their start and end apart: 64, of which 21 were waited for; matrix products, arithmetic and copies ran while one was open for 30% of the time, Pallas kernels for 0%

commit v1 on v0

v1 whole, which is shorter than its diff:
```python
import functools

import jax
import jax.numpy as jnp
from jax import lax
from jax.experimental import pallas as pl
from jax.experimental.pallas import tpu as pltpu
from jax.sharding import PartitionSpec as P

MESH = pl.DeviceIdType.MESH
TICKS = 16
K = 4
ROUNDS = TICKS // K
CH = 4
TILES = 5
TOP = 8
ROWS = 56
PAD = 5
HIGHEST = lax.Precision.HIGHEST

DIRS = ((-1, 0), (1, 0), (0, -1), (0, 1), (-1, -1), (1, -1), (-1, 1), (1, 1))
OPPOSITE = (1, 0, 3, 2, 7, 6, 5, 4)


def lanes_roll(v, shift):
    if isinstance(shift, int):
        shift = shift % 128
        return v if shift == 0 else pltpu.roll(v, shift, 1)
    return pltpu.roll(v, lax.rem(shift + 256, 128), 1)


def rows_roll(v, shift):
    return pltpu.roll(v, shift % 8, 0)


def tile_rows(xt):
    return pl.ds(TOP + 8 * xt, 8)


def kernel(
    n_gx, n_gy, nz,
    e_in, h_in, f_in, material_in, inverse, rate, partial, profile_in, offset, start, length,
    e_out, h_out, g_out,
    eh, coup, fwd, grad, labels, strip, strip_c, strip_j, own_pack,
    send_y, send_c, recv_x, recv_y, recv_c,
    w_send, w_all, profile, j_flat, j_all, j_now, v_send, v_recv, c_recv, inject_a, inject_b,
    load_sem, ssem, rsem, w_ssem, w_rsem, p_ssem, p_rsem, c_ssem, c_rsem, v_ssem, v_rsem,
):
    chunks = nz // CH
    gx = lax.axis_index("gx")
    gy = lax.axis_index("gy")
    f32 = jnp.float32
    lane = lax.broadcasted_iota(jnp.int32, (8, 128), 1)
    sub = lax.broadcasted_iota(jnp.int32, (8, 128), 0)
    group = lane // 8
    place = lane - group * 8
    low_half = place < 4
    zero = jnp.zeros((8, 128), f32)
    own_rows = pl.ds(TOP + 4, 32)

    exists = []
    devices = []
    for dx, dy in DIRS:
        ok = None
        for d, p, n in ((dx, gx, n_gx), (dy, gy, n_gy)):
            if d:
                here = (p > 0) if d < 0 else (p < n - 1)
                ok = here if ok is None else jnp.logical_and(ok, here)
        exists.append(ok)
        devices.append((gx + dx, gy + dy))

    def clear(zi, carry):
        for c in range(6):
            for row in (0, 8, 40, 48):
                eh[c, zi, pl.ds(row, 8), :] = zero
            strip[c, zi] = zero
        for row in (8, 40):
            labels[zi, pl.ds(row, 8), :] = jnp.full((8, 128), 4, jnp.int32)
            for c in range(3):
                fwd[c, zi, pl.ds(row, 8), :] = zero
        for xt in range(TILES):
            grad[zi, tile_rows(xt), :] = zero
            j_now[zi, pl.ds(8 * xt, 8), :] = zero
        strip_c[zi] = zero
        for c in range(2):
            strip_j[c, zi] = zero
        return carry

    lax.fori_loop(0, nz + 2 * PAD, clear, 0)
    for zi in [*range(PAD), *range(nz + PAD, nz + 2 * PAD)]:
        for row in range(16, 40, 8):
            for c in range(6):
                eh[c, zi, pl.ds(row, 8), :] = zero
            for c in range(3):
                fwd[c, zi, pl.ds(row, 8), :] = zero
        for xt in range(TILES):
            coup[zi, tile_rows(xt), :] = zero

    planes = pl.ds(PAD, nz)
    loads = [
        pltpu.make_async_copy(e_in, eh.at[pl.ds(0, 3), planes, own_rows, :], load_sem.at[1]),
        pltpu.make_async_copy(h_in, eh.at[pl.ds(3, 3), planes, own_rows, :], load_sem.at[2]),
        pltpu.make_async_copy(material_in, labels.at[planes, own_rows, :], load_sem.at[3]),
        pltpu.make_async_copy(profile_in, profile.at[:, pl.ds(4 * nz, 32 * nz)], load_sem.at[4]),
        pltpu.make_async_copy(f_in, fwd.at[:, planes, own_rows, :], load_sem.at[5]),
    ]
    for load in loads:
        load.start()

    def clear_received(z, carry):
        for par in range(2):
            for c in range(6):
                recv_x[par, c, z] = zero
            for d in range(2):
                recv_y[par, d, z] = zero
        for d in range(2):
            v_recv[d, z] = zero
        c_recv[z] = zero
        return carry

    lax.fori_loop(0, nz, clear_received, 0)
    for q in range(chunks):
        for par in range(2):
            for d in range(2):
                recv_c[par, d, q] = zero
    for m in range(8):
        profile[pl.ds(8 * m, 8), pl.ds(0, 4 * nz)] = jnp.zeros((8, 4 * nz), f32)
        profile[pl.ds(8 * m, 8), pl.ds(36 * nz, 4 * nz)] = jnp.zeros((8, 4 * nz), f32)

    barrier = pltpu.get_barrier_semaphore()
    for j in range(1, n_gx):
        peer = (lax.rem(gx + j, n_gx), gy)
        pl.semaphore_signal(barrier, inc=1, device_id=peer, device_id_type=MESH)
    for d in range(2, 8):
        @pl.when(exists[d])
        def _():
            pl.semaphore_signal(barrier, inc=1, device_id=devices[d], device_id_type=MESH)
    one = lambda flag: jnp.where(flag, 1, 0)
    near_x = one(exists[0]) + one(exists[1])
    near_y = one(exists[2]) + one(exists[3])
    pl.semaphore_wait(barrier, n_gx - 1 + near_y * (1 + near_x))

    def remote(src, dst, send, recv, d):
        return pltpu.make_async_remote_copy(
            src_ref=src, dst_ref=dst, send_sem=send, recv_sem=recv,
            device_id=devices[d], device_id_type=MESH,
        )

    def start_if(d, copy):
        @pl.when(exists[d])
        def _():
            copy.start()

    def wait_if(d, copy):
        @pl.when(exists[d])
        def _():
            copy.wait()

    row = lax.broadcasted_iota(jnp.int32, (32, 128), 0)
    tick = (4 * (row - (row // 4) * 4) + row // 8).astype(f32)
    radians = tick * rate[...]
    cosine = jnp.cos(radians)
    sine = jnp.sin(radians)
    cosine = jnp.concatenate([cosine] * 4, axis=0)
    sine = jnp.concatenate([sine] * 4, axis=0)
    dims = (((1,), (1,)), ((), ()))
    term = lax.dot_general(partial[0], cosine, dims, precision=HIGHEST, preferred_element_type=f32)
    term = term - lax.dot_general(
        partial[1], sine, dims, precision=HIGHEST, preferred_element_type=f32
    )
    packed = zero
    for g in range(4):
        packed = jnp.where(lane // 32 == g, term[8 * g : 8 * g + 8], packed)
    w_send[...] = packed

    def w_copy(j, slot, sem_slot):
        peer = (lax.rem(gx + j, n_gx), gy)
        return pltpu.make_async_remote_copy(
            src_ref=w_send, dst_ref=w_all.at[slot], send_sem=w_ssem.at[sem_slot],
            recv_sem=w_rsem.at[sem_slot], device_id=peer, device_id_type=MESH,
        )

    for j in range(1, n_gx):
        w_copy(j, j, j).start()

    def p_copy(d):
        src = profile_in.at[:, pl.ds(0 if d == 0 else 28 * nz, 4 * nz)]
        dst = profile.at[:, pl.ds(36 * nz if d == 0 else 0, 4 * nz)]
        return remote(src, dst, p_ssem.at[d], p_rsem.at[OPPOSITE[d]], d)

    def p_wait(d):
        src = profile_in.at[:, pl.ds(0, 4 * nz)]
        dst = profile.at[:, pl.ds(0 if d == 0 else 36 * nz, 4 * nz)]
        return remote(src, dst, p_ssem.at[d], p_rsem.at[d], d)

    for d in range(2):
        start_if(d, p_copy(d))

    def message(d, q, par, arriving):
        z0 = pl.multiple_of(q * CH, CH)
        zs = pl.ds(z0, CH)
        sem = rsem.at[par, d if arriving else OPPOSITE[d], q]
        if d < 2:
            lower = (d == 0) == arriving
            dst = recv_x.at[par, :, zs, pl.ds(0 if lower else 4, 4), :]
            src = eh.at[:, pl.ds(z0 + PAD, CH), pl.ds(TOP + 4 if d == 0 else TOP + 32, 4), :]
        elif d < 4:
            dst = recv_y.at[par, (d - 2) if arriving else (3 - d), zs]
            src = send_y.at[d - 2, zs]
        else:
            side = (d - 4) // 2
            dx = DIRS[d][0]
            out = pl.ds(4 if dx < 0 else 0, 4)
            into = pl.ds(4 if (dx > 0) == arriving else 0, 4)
            dst = recv_c.at[par, side if arriving else 1 - side, q, into, :]
            src = send_c.at[side, q, out, :]
        return remote(src, dst, ssem.at[d, q], sem, d)

    def pack_and_send(q, par):
        corner = [zero, zero]
        for i in range(CH):
            z = q * CH + i
            zi = z + PAD
            packs = []
            for half in range(2):
                acc = zero
                for c in range(3):
                    for xt in range(TILES):
                        v = eh[3 * half + c, zi, tile_rows(xt), :]
                        acc = jnp.where(
                            group == 5 * c + xt, lanes_roll(v, 40 * c + 8 * xt + 4), acc
                        )
                own_pack[half, z] = acc
                packs.append(acc)
            pe, ph = packs
            down = jnp.where(low_half, lanes_roll(ph, -4), pe)
            up = jnp.where(low_half, pe, lanes_roll(ph, 4))
            for side, v in ((0, down), (1, up)):
                send_y[side, z] = v
                moved = jnp.where(sub < 4, lanes_roll(v, 8 * i - 32), lanes_roll(v, 8 * i))
                here = (group == i) | (group == 5 + i) | (group == 10 + i)
                corner[side] = jnp.where(here, moved, corner[side])
        for side in range(2):
            send_c[side, q] = corner[side]
        for d in range(8):
            start_if(d, message(d, q, par, False))

    xt0 = ((group == 0) | (group == 5) | (group == 10)) & (sub < 4)
    xt4 = ((group == 4) | (group == 9) | (group == 14)) & (sub >= 4)

    def unpack(q, par, r):
        for i in range(CH):
            z = q * CH + i
            zi = z + PAD
            packs = []
            for half in range(2):
                acc = own_pack[half, z]
                for c in range(3):
                    v = recv_x[par, 3 * half + c, z]
                    old = eh[3 * half + c, zi, tile_rows(0), :]
                    eh[3 * half + c, zi, tile_rows(0), :] = jnp.where(sub < 4, v, old)
                    old = eh[3 * half + c, zi, tile_rows(4), :]
                    eh[3 * half + c, zi, tile_rows(4), :] = jnp.where(sub < 4, old, v)
                    acc = jnp.where((group == 5 * c) & (sub < 4), lanes_roll(v, 40 * c + 4), acc)
                    acc = jnp.where(
                        (group == 5 * c + 4) & (sub >= 4), lanes_roll(v, 40 * c + 36), acc
                    )
                packs.append(acc)
            pe, ph = packs
            sides = []
            for side in range(2):
                v = recv_y[par, side, z]
                x = recv_c[par, side, q]
                v = jnp.where(xt0, lanes_roll(x, -8 * i), v)
                v = jnp.where(xt4, lanes_roll(x, 32 - 8 * i), v)
                sides.append(v)
            from_down, from_up = sides
            right = (
                jnp.where(low_half, pe, from_up),
                jnp.where(low_half, ph, lanes_roll(from_up, 4)),
            )
            left = (
                jnp.where(low_half, from_down, pe),
                jnp.where(low_half, lanes_roll(from_down, -4), ph),
            )
            for half in range(2):
                for c in range(3):
                    strip[3 * half + c, zi] = jnp.where(
                        lane < 64,
                        lanes_roll(right[half], -40 * c),
                        lanes_roll(left[half], 64 - 40 * c),
                    )
            for xt in range(TILES):
                j_now[zi, pl.ds(8 * xt, 8), :] = lanes_roll(j_all[z, pl.ds(8 * xt, 8), :], -r)
            for c in range(2):
                a = lanes_roll(inject_a[z], 6 - 4 * c - r)
                b = lanes_roll(inject_b[z], 1 - 4 * c - r)
                strip_j[c, zi] = jnp.where(place == 6, a, jnp.where(place == 1, b, zero))

    loads[0].wait()
    loads[1].wait()

    def first_chunk(q, carry):
        pack_and_send(q, 0)
        return carry

    lax.fori_loop(0, chunks, first_chunk, 0)

    loads[2].wait()

    def couple(z, carry):
        zi = z + PAD
        for xt in range(TILES):
            label = labels[zi, tile_rows(xt), :]
            value = zero
            for n in range(4):
                value = jnp.where(label == n, 0.5 * inverse[n], value)
            coup[zi, tile_rows(xt), :] = value
        return carry

    lax.fori_loop(0, nz, couple, 0)

    def c_copy(d, arriving):
        lower = (d == 0) == arriving
        src = coup.at[planes, pl.ds(TOP + 4 if d == 0 else TOP + 32, 4), :]
        dst = c_recv.at[:, pl.ds(0 if lower else 4, 4), :]
        return remote(src, dst, c_ssem.at[d], c_rsem.at[d if arriving else OPPOSITE[d]], d)

    for d in range(2):
        start_if(d, c_copy(d, False))

    total = w_send[...]
    for j in range(1, n_gx):
        w_copy(j, j, j).wait()
        total = total + w_all[j]
    loads[3].wait()
    for d in range(2):
        @pl.when(exists[d])
        def _():
            p_copy(d).wait_send()
            p_wait(d).wait_recv()
    parts = []
    for c in range(2):
        for g in range(4):
            keep = (lane < 32) & (lax.rem(lane // 4, 2) == c)
            parts.append(jnp.where(keep, lanes_roll(total, -32 * g), zero))
    weights = jnp.concatenate(parts, axis=0)
    first = start[0]
    last = start[0] + length[0]
    for xt in range(TILES):
        cells = pl.ds(8 * nz * xt, 8 * nz)
        now = lax.dot_general(
            profile[:, cells], weights, (((0,), (0,)), ((), ())),
            precision=HIGHEST, preferred_element_type=f32,
        )
        x = gx * 32 - 4 + 8 * xt + lax.broadcasted_iota(jnp.int32, (8 * nz, 128), 0) // nz
        j_flat[cells, :] = jnp.where((x >= first) & (x < last), now, 0.0)

    for d in range(2):
        wait_if(d, c_copy(d, True))
    where_at = offset[0]

    def prepare(z, carry):
        zi = z + PAD
        halo = c_recv[z]
        coup[zi, tile_rows(0), :] = jnp.where(sub < 4, halo, coup[zi, tile_rows(0), :])
        coup[zi, tile_rows(4), :] = jnp.where(sub < 4, coup[zi, tile_rows(4), :], halo)
        acc = zero
        for xt in range(TILES):
            v = coup[zi, tile_rows(xt), :]
            acc = jnp.where(group == xt, lanes_roll(v, 8 * xt + 4), acc)
            j = j_flat[pl.ds(z + 8 * nz * xt, 8, stride=nz), :]
            j_all[z, pl.ds(8 * xt, 8), :] = j
            acc = jnp.where(group == 5 + xt, lanes_roll(j, 40 + 8 * xt), acc)
        v_send[0, z] = jnp.where((lane >= 40) & (where_at != 2), 0.0, acc)
        v_send[1, z] = jnp.where((lane >= 40) & (where_at != 125), 0.0, acc)
        return carry

    lax.fori_loop(0, nz, prepare, 0)

    def v_copy(d, arriving):
        return remote(
            v_send.at[d - 2], v_recv.at[(d - 2) if arriving else (3 - d)],
            v_ssem.at[d - 2], v_rsem.at[(d - 2) if arriving else (3 - d)], d,
        )

    for d in (2, 3):
        start_if(d, v_copy(d, False))
    for d in (2, 3):
        wait_if(d, v_copy(d, True))

    def finish(z, carry):
        zi = z + PAD
        own_down, own_up = v_send[0, z], v_send[1, z]
        from_down, from_up = v_recv[0, z], v_recv[1, z]
        right = jnp.where(low_half, own_up, from_up)
        left = jnp.where(low_half, from_down, own_up)
        strip_c[zi] = jnp.where(lane < 64, right, lanes_roll(left, 64))
        inject_a[z] = jnp.where(lane < 64, lanes_roll(from_up, -40), lanes_roll(own_down, 24))
        inject_b[z] = jnp.where(lane < 64, lanes_roll(own_up, -40), lanes_roll(from_down, 24))
        return carry

    lax.fori_loop(0, nz, finish, 0)
    loads[4].wait()

    half = jnp.full((8, 128), 0.5, f32)
    outside_x = (sub < 4) & (gx == 0)
    half_first = jnp.where(outside_x, 0.0, half)
    outside = (outside_x & ((group == 0) | (group == 8))) | (
        (lane >= 64) & low_half & (gy == 0)
    )
    half_strip = jnp.where(outside, 0.0, half)
    on_sheet = lane == where_at

    def up_rows(v):
        return rows_roll(jnp.where(sub == 0, lanes_roll(v, -8), v), -1)

    def down_rows(v):
        return rows_roll(jnp.where(sub == 7, lanes_roll(v, 8), v), 1)

    def plane_step(z, s):
        zi = z + PAD
        inside = z >= 0
        k_strip = jnp.where(inside, half_strip, 0.0)
        k_first = jnp.where(inside, half_first, 0.0)
        k_rest = jnp.where(inside, half, 0.0)
        sx, sy, sz, tx, ty, tz = [strip[c, zi] for c in range(6)]
        sx_up, sy_up = strip[0, zi + 1], strip[1, zi + 1]
        tx_dn, ty_dn = strip[3, zi - 1], strip[4, zi - 1]
        ux = tx - k_strip * ((lanes_roll(sz, -1) - sz) - (sy_up - sy))
        uy = ty - k_strip * ((sx_up - sx) - (up_rows(sz) - sz))
        uz = tz - k_strip * ((up_rows(sy) - sy) - (lanes_roll(sx, -1) - sx))
        c = strip_c[zi]
        vx = sx + c * ((uz - lanes_roll(uz, 1)) - (uy - ty_dn))
        vy = sy + c * ((ux - tx_dn) - (uz - down_rows(uz)))
        vz = sz + c * ((uy - down_rows(uy)) - (ux - lanes_roll(ux, 1)))
        if s == 0:
            vx = vx + strip_j[0, zi]
            vz = vz + strip_j[1, zi]
        for n, v in enumerate((vx, vy, vz, ux, uy, uz)):
            strip[n, zi] = v
        for xt in range(TILES):
            rows = tile_rows(xt)
            above = pl.ds(TOP + 8 * xt + 1, 8)
            below = pl.ds(TOP + 8 * xt - 1, 8)
            k = k_first if xt == 0 else k_rest
            ex, ey, ez = [eh[n, zi, rows, :] for n in range(3)]
            hx, hy, hz = [eh[n, zi, rows, :] for n in range(3, 6)]
            ex_up, ey_up = eh[0, zi + 1, rows, :], eh[1, zi + 1, rows, :]
            ey_x, ez_x = eh[1, zi, above, :], eh[2, zi, above, :]
            turn = 127 - (8 * xt + 4)
            ex_y = jnp.where(lane == 127, lanes_roll(sx, turn), lanes_roll(ex, -1))
            ez_y = jnp.where(lane == 127, lanes_roll(sz, turn), lanes_roll(ez, -1))
            hx = hx - k * ((ez_y - ez) - (ey_up - ey))
            hy = hy - k * ((ex_up - ex) - (ez_x - ez))
            hz = hz - k * ((ey_x - ey) - (ex_y - ex))
            eh[3, zi, rows, :] = hx
            eh[4, zi, rows, :] = hy
            eh[5, zi, rows, :] = hz
            hx_dn, hy_dn = eh[3, zi - 1, rows, :], eh[4, zi - 1, rows, :]
            hy_x, hz_x = eh[4, zi, below, :], eh[5, zi, below, :]
            turn = -(64 + 8 * xt + 3)
            hx_y = jnp.where(lane == 0, lanes_roll(ux, turn), lanes_roll(hx, 1))
            hz_y = jnp.where(lane == 0, lanes_roll(uz, turn), lanes_roll(hz, 1))
            cc = coup[zi, rows, :]
            jx = jnp.broadcast_to(j_now[zi, pl.ds(8 * xt, 8), pl.ds(8 * s, 1)], (8, 128))
            jz = jnp.broadcast_to(j_now[zi, pl.ds(8 * xt, 8), pl.ds(8 * s + 4, 1)], (8, 128))
            ex = ex + cc * ((hz - hz_y) - (hy - hy_dn)) + jnp.where(on_sheet, jx, 0.0)
            ey = ey + cc * ((hx - hx_dn) - (hz - hz_x))
            ez = ez + cc * ((hy - hy_x) - (hx - hx_y)) + jnp.where(on_sheet, jz, 0.0)
            eh[0, zi, rows, :] = ex
            eh[1, zi, rows, :] = ey
            eh[2, zi, rows, :] = ez
            grad[zi, rows, :] = grad[zi, rows, :] + (
                ex * fwd[0, zi, rows, :] + ey * fwd[1, zi, rows, :] + ez * fwd[2, zi, rows, :]
            )

    def one_round(r, carry):
        par = lax.rem(r, 2)
        later = lax.rem(r + 1, 2)

        def one_chunk(q, carry):
            @pl.when(q < chunks)
            def _():
                for d in range(8):
                    wait_if(d, message(d, q, par, True))
                unpack(q, par, r)

            def wave(i, carry):
                w = q * CH - 1 + i
                for s in range(K):
                    plane_step(w - s, s)
                return carry

            lax.fori_loop(0, CH, wave, 0)

            @pl.when(jnp.logical_and(q > 0, r < ROUNDS - 1))
            def _():
                pack_and_send(q - 1, later)

            return carry

        return lax.fori_loop(0, chunks + 1, one_chunk, carry)

    lax.fori_loop(0, ROUNDS, one_round, 0)

    stores = [
        pltpu.make_async_copy(eh.at[pl.ds(0, 3), planes, own_rows, :], e_out, load_sem.at[1]),
        pltpu.make_async_copy(eh.at[pl.ds(3, 3), planes, own_rows, :], h_out, load_sem.at[2]),
        pltpu.make_async_copy(grad.at[planes, own_rows, :], g_out, load_sem.at[3]),
    ]
    for store in stores:
        store.start()
    for store in stores:
        store.wait()


def shards(n_gx, n_gy, *args):
    (electric, magnetic, forward_field, material, inv_permittivity, spectral_rate,
     intersection_partial, mode_profile, sheet_offset, plane_start, monitor_length) = args
    nz = electric.shape[1]
    f32 = jnp.float32
    zp = nz + 2 * PAD
    chunks = nz // CH
    dma = pltpu.SemaphoreType.DMA
    vmem = lambda *shape: pltpu.VMEM(shape, f32)
    anyspace = pl.BlockSpec(memory_space=pl.ANY)
    smem = pl.BlockSpec(memory_space=pltpu.SMEM)
    vm = pl.BlockSpec(memory_space=pltpu.VMEM)
    e, h, g = pl.pallas_call(
        functools.partial(kernel, n_gx, n_gy, nz),
        out_shape=[
            jax.ShapeDtypeStruct(electric.shape, f32),
            jax.ShapeDtypeStruct(electric.shape, f32),
            jax.ShapeDtypeStruct(material.shape, f32),
        ],
        in_specs=[anyspace, anyspace, anyspace, anyspace, smem, vm, vm, anyspace, smem, smem, smem],
        out_specs=[anyspace] * 3,
        scratch_shapes=[
            vmem(6, zp, ROWS, 128),
            vmem(zp, ROWS, 128),
            vmem(3, zp, ROWS, 128),
            vmem(zp, ROWS, 128),
            pltpu.VMEM((zp, ROWS, 128), jnp.int32),
            vmem(6, zp, 8, 128),
            vmem(zp, 8, 128),
            vmem(2, zp, 8, 128),
            vmem(2, nz, 8, 128),
            vmem(2, nz, 8, 128),
            vmem(2, chunks, 8, 128),
            vmem(2, 6, nz, 8, 128),
            vmem(2, 2, nz, 8, 128),
            vmem(2, 2, chunks, 8, 128),
            vmem(8, 128),
            vmem(n_gx, 8, 128),
            vmem(64, 40 * nz),
            vmem(40 * nz, 128),
            vmem(nz, 40, 128),
            vmem(zp, 40, 128),
            vmem(2, nz, 8, 128),
            vmem(2, nz, 8, 128),
            vmem(nz, 8, 128),
            vmem(nz, 8, 128),
            vmem(nz, 8, 128),
            dma((6,)),
            dma((8, chunks)),
            dma((2, 8, chunks)),
            dma((n_gx,)),
            dma((n_gx,)),
            dma((2,)),
            dma((2,)),
            dma((2,)),
            dma((2,)),
            dma((2,)),
            dma((2,)),
        ],
        compiler_params=pltpu.CompilerParams(
            collective_id=0, has_side_effects=True, vmem_limit_bytes=56 << 20
        ),
    )(
        electric, magnetic, forward_field, material, inv_permittivity,
        spectral_rate.reshape(1, -1), intersection_partial,
        mode_profile.reshape(-1, mode_profile.shape[2]),
        sheet_offset, plane_start, monitor_length,
    )
    return e, h, g * (1.0 / TICKS)


def solution(mesh):
    placed = (
        P(None, None, "gx", "gy"),
        P(None, None, "gx", "gy"),
        P(None, None, "gx", "gy"),
        P(None, "gx", "gy"),
        P(),
        P(),
        P("gx", "gy", None),
        P("gy", None, "gx"),
        P("gy"),
        P("gy"),
        P("gy"),
    )
    return jax.shard_map(
        functools.partial(shards, mesh.shape["gx"], mesh.shape["gy"]),
        mesh=mesh,
        in_specs=placed,
        out_specs=(P(None, None, "gx", "gy"), P(None, None, "gx", "gy"), P(None, "gx", "gy")),
        check_vma=False,
    )
```

time: 807 us -> 233 us (0.29)
  local copies, waits for them, and re-layouts: 317 us -> 3.93 us
  starting transfers between devices: 255 us -> 0 us
  Pallas kernels: 0 us -> 220 us
  other arithmetic: 122 us -> 1.88 us
  blocking collectives: 59.6 us -> 0 us
  waiting for transfers between devices: 33.5 us -> 0 us
    ppermute x64 -> x0, starting transfers between devices: 255 us -> none  [shifted(): return lax.ppermute(block, axis, route)]
    pallas_call x0 -> x1, Pallas kernels: none -> 220 us  [shards(): pl.pallas_call(functools.partial(kernel, n_gx, n_gy, nz), out_shape=[jax....]
    slice x258 -> x0, local copies, waits for them, and re-layouts: 200 us -> none  [the longest x96 86.1 us: ahead(): rest = lax.slice_in_dim(field, 1, size, axis=along_axis)]
    squeeze x211 -> x0, local copies, waits for them, and re-layouts: 88 us -> none  [the longest x32 21.7 us: update_magnetic(): ghost_y[0]]
    psum x1 -> x0, blocking collectives: 59.6 us -> none  [shards(): cotangent = lax.psum(intersection_partial, 'gx')]
    add x16 -> x0, other arithmetic: 59.2 us -> none  [accumulate(): total + (electric[0] * forward_field[0] + electric[1] * forward_field[1]...]
    sub x16 -> x0, other arithmetic: 48.1 us -> none  [update_magnetic(): magnetic[1]]
    ppermute x64 -> x0, waiting for transfers between devices: 33.5 us -> none  [shifted(): return lax.ppermute(block, axis, route)]
  transfers between devices with their start and end apart: 64 -> 0, of which waited for: 21 -> 0; matrix products, arithmetic and copies ran while one was open for 30% -> 0% of each run, Pallas kernels for 0% -> 0%
where the time goes in v1:
time: 233 us; the launch traced here: 228 us
  Pallas kernels  220 us (94%)
  local copies, waits for them, and re-layouts  3.93 us (2%)
  between operations  2.58 us (1%)
    pallas_call x1, Pallas kernels, shards(): pl.pallas_call(functools.partial(kernel, n_gx, n_gy, nz), out_shape=[jax....  220 us

profile of v1, /device:TPU:33, one launch (start us, length us, event | category | flops | bytes accessed | tf_op | source)
XLA Modules:
  0.0 228.3 jit_solution(17753858341529630597)
XLA Ops:
  2.6 219.9 %shard_map.130 = (f32[3,32,32,128]{3,2,1,0:T(8,128)}, f32[3,32,32,128]{3,2,1,0:T(8,128)}, f32[32,32,128]{2,1,0:T(8,128)}) custom-call(f32[3,32,32,128]{3,2,1,0:T(8,128)} %e_in.1, f32[3,32,32,128]{3,2,1,0:T(8,128)} %h_in.1, f32[3,32,32,128]{3,2,1,0:T(8,128)} %f_in.1, s32[32,32,128]{2,1,0:T(8,128)} %material_in.1, f32[4]{0:T(128)} %inverse.1, ...), custom_call_target="tpu_custom_call" | custom-call | tf_op jit(solution)/shard_map/pallas_call | solution.py:530
  222.5 1.9 broadcast_multiply_fusion
  224.4 0.0 copy-start
  224.4 2.8 %copy.19 = f32[3,32,32,128]{3,2,1,0:T(8,128)} copy(f32[3,32,32,128]{3,2,1,0:T(8,128)} %get-tuple-element.12) | data formatting | bytes 3145728
  227.1 0.0 copy-done
  227.2 1.1 copy.20
Async XLA Ops:
  224.4 2.8 %copy-start = (f32[3,32,32,128]{3,2,1,0:T(8,128)S(1)}, f32[3,32,32,128]{3,2,1,0:T(8,128)}, u32[]{:S(2)}) copy-start(f32[3,32,32,128]{3,2,1,0:T(8,128)} %get-tuple-element.13) | copy-start | bytes 4718596

commit v2 on v1

v2 whole, which is shorter than its diff:
```python
import functools

import jax
import jax.numpy as jnp
from jax import lax
from jax.experimental import pallas as pl
from jax.experimental.pallas import tpu as pltpu
from jax.sharding import PartitionSpec as P

MESH = pl.DeviceIdType.MESH
TICKS = 16
K = 4
ROUNDS = TICKS // K
CH = 4
TILES = 5
TOP = 8
ROWS = 56
PAD = 1
EXTRA = 5
HIGHEST = lax.Precision.HIGHEST

DIRS = ((-1, 0), (1, 0), (0, -1), (0, 1), (-1, -1), (1, -1), (-1, 1), (1, 1))
OPPOSITE = (1, 0, 3, 2, 7, 6, 5, 4)


def lanes_roll(v, shift):
    if isinstance(shift, int):
        shift = shift % 128
        return v if shift == 0 else pltpu.roll(v, shift, 1)
    return pltpu.roll(v, lax.rem(shift + 256, 128), 1)


def rows_roll(v, shift):
    return pltpu.roll(v, shift % 8, 0)


def tile_rows(xt):
    return pl.ds(TOP + 8 * xt, 8)


def kernel(
    n_gx, n_gy, nz,
    e_in, h_in, f_in, material_in, inverse, rate, partial, profile_in, offset, start, length,
    e_out, h_out, g_out,
    eh, e0, h0, e1, h1, e2, h2, e3, h3, strip0, strip1, strip2, strip3,
    grad0, grad1, grad2, grad3, coup, fwd, labels, strip_c, strip_j, own_pack,
    send_y, send_c, recv_x, recv_y, recv_c,
    w_send, w_all, profile, j_flat, j_all, pick, v_send, v_recv, c_recv, inject_a, inject_b,
    load_sem, out_sem, ssem, rsem, w_ssem, w_rsem, p_ssem, p_rsem, c_ssem, c_rsem, v_ssem, v_rsem,
):
    chunks = nz // CH
    gx = lax.axis_index("gx")
    gy = lax.axis_index("gy")
    f32 = jnp.float32
    lane = lax.broadcasted_iota(jnp.int32, (8, 128), 1)
    sub = lax.broadcasted_iota(jnp.int32, (8, 128), 0)
    group = lane // 8
    place = lane - group * 8
    low_half = place < 4
    zero = jnp.zeros((8, 128), f32)
    own_rows = pl.ds(TOP + 4, 32)

    exists = []
    devices = []
    for dx, dy in DIRS:
        ok = None
        for d, p, n in ((dx, gx, n_gx), (dy, gy, n_gy)):
            if d:
                here = (p > 0) if d < 0 else (p < n - 1)
                ok = here if ok is None else jnp.logical_and(ok, here)
        exists.append(ok)
        devices.append((gx + dx, gy + dy))

    e_at = (e0, e1, e2, e3)
    h_at = (h0, h1, h2, h3, eh)
    strip_at = (strip0, strip1, strip2, strip3)
    grads = (grad0, grad1, grad2, grad3)

    planes = pl.ds(PAD, nz)
    loads = [
        pltpu.make_async_copy(e_in, eh.at[pl.ds(0, 3), planes, own_rows, :], load_sem.at[1]),
        pltpu.make_async_copy(h_in, eh.at[pl.ds(3, 3), planes, own_rows, :], load_sem.at[2]),
        pltpu.make_async_copy(material_in, labels.at[planes, own_rows, :], load_sem.at[3]),
        pltpu.make_async_copy(profile_in, profile.at[:, pl.ds(4 * nz, 32 * nz)], load_sem.at[4]),
        pltpu.make_async_copy(f_in, fwd.at[:, planes, own_rows, :], load_sem.at[5]),
    ]
    for load in loads:
        load.start()

    for c in range(3):
        for xt in range(TILES):
            eh[3 + c, 0, tile_rows(xt), :] = zero
    for level in range(K):
        for c in range(3):
            for xt in range(TILES):
                h_at[level][c, 0, tile_rows(xt), :] = zero
                e_at[level][c, nz + PAD, tile_rows(xt), :] = zero
            strip_at[level][3 + c, 0] = zero
            strip_at[level][c, nz + PAD] = zero

    def clear(zi, carry):
        for total in grads:
            for xt in range(TILES):
                total[zi, tile_rows(xt), :] = zero
        return carry

    lax.fori_loop(PAD, nz + PAD, clear, 0)

    def clear_x(side):
        rows = pl.ds(4 * side, 4)
        none = jnp.zeros((4, 128), f32)

        def at(z, carry):
            for par in range(2):
                for c in range(6):
                    recv_x[par, c, z, rows, :] = none
            c_recv[z, rows, :] = none
            return carry

        lax.fori_loop(0, nz, at, 0)
        edge = jnp.zeros((64, 4 * nz), f32)
        profile[:, pl.ds(36 * nz * side, 4 * nz)] = edge

    def clear_y(side):
        def at(z, carry):
            for par in range(2):
                recv_y[par, side, z] = zero
            v_recv[side, z] = zero
            return carry

        lax.fori_loop(0, nz, at, 0)

    for side in range(2):
        @pl.when(jnp.logical_not(exists[side]))
        def _():
            clear_x(side)

        @pl.when(jnp.logical_not(exists[2 + side]))
        def _():
            clear_y(side)

    for d in range(4, 8):
        rows = pl.ds(4 if DIRS[d][0] > 0 else 0, 4)

        @pl.when(jnp.logical_not(exists[d]))
        def _():
            for par in range(2):
                for q in range(chunks):
                    recv_c[par, (d - 4) // 2, q, rows, :] = jnp.zeros((4, 128), f32)

    barrier = pltpu.get_barrier_semaphore()
    for j in range(1, n_gx):
        peer = (lax.rem(gx + j, n_gx), gy)
        pl.semaphore_signal(barrier, inc=1, device_id=peer, device_id_type=MESH)
    for d in range(2, 8):
        @pl.when(exists[d])
        def _():
            pl.semaphore_signal(barrier, inc=1, device_id=devices[d], device_id_type=MESH)
    one = lambda flag: jnp.where(flag, 1, 0)
    near_x = one(exists[0]) + one(exists[1])
    near_y = one(exists[2]) + one(exists[3])
    pl.semaphore_wait(barrier, n_gx - 1 + near_y * (1 + near_x))

    def remote(src, dst, send, recv, d):
        return pltpu.make_async_remote_copy(
            src_ref=src, dst_ref=dst, send_sem=send, recv_sem=recv,
            device_id=devices[d], device_id_type=MESH,
        )

    def start_if(d, copy):
        @pl.when(exists[d])
        def _():
            copy.start()

    def wait_if(d, copy):
        @pl.when(exists[d])
        def _():
            copy.wait()

    row = lax.broadcasted_iota(jnp.int32, (32, 128), 0)
    tick = (4 * (row - (row // 4) * 4) + row // 8).astype(f32)
    radians = tick * rate[...]
    cosine = jnp.cos(radians)
    sine = jnp.sin(radians)
    cosine = jnp.concatenate([cosine] * 4, axis=0)
    sine = jnp.concatenate([sine] * 4, axis=0)
    dims = (((1,), (1,)), ((), ()))
    term = lax.dot_general(partial[0], cosine, dims, precision=HIGHEST, preferred_element_type=f32)
    term = term - lax.dot_general(
        partial[1], sine, dims, precision=HIGHEST, preferred_element_type=f32
    )
    packed = zero
    for g in range(4):
        packed = jnp.where(lane // 32 == g, term[8 * g : 8 * g + 8], packed)
    w_send[...] = packed

    def w_copy(j, slot, sem_slot):
        peer = (lax.rem(gx + j, n_gx), gy)
        return pltpu.make_async_remote_copy(
            src_ref=w_send, dst_ref=w_all.at[slot], send_sem=w_ssem.at[sem_slot],
            recv_sem=w_rsem.at[sem_slot], device_id=peer, device_id_type=MESH,
        )

    for j in range(1, n_gx):
        w_copy(j, j, j).start()

    def p_copy(d):
        src = profile_in.at[:, pl.ds(0 if d == 0 else 28 * nz, 4 * nz)]
        dst = profile.at[:, pl.ds(36 * nz if d == 0 else 0, 4 * nz)]
        return remote(src, dst, p_ssem.at[d], p_rsem.at[OPPOSITE[d]], d)

    def p_wait(d):
        src = profile_in.at[:, pl.ds(0, 4 * nz)]
        dst = profile.at[:, pl.ds(0 if d == 0 else 36 * nz, 4 * nz)]
        return remote(src, dst, p_ssem.at[d], p_rsem.at[d], d)

    for d in range(2):
        start_if(d, p_copy(d))

    def message(d, q, par, arriving):
        z0 = pl.multiple_of(q * CH, CH)
        zs = pl.ds(z0, CH)
        sem = rsem.at[par, d if arriving else OPPOSITE[d], q]
        if d < 2:
            lower = (d == 0) == arriving
            dst = recv_x.at[par, :, zs, pl.ds(0 if lower else 4, 4), :]
            src = eh.at[:, pl.ds(z0 + PAD, CH), pl.ds(TOP + 4 if d == 0 else TOP + 32, 4), :]
        elif d < 4:
            dst = recv_y.at[par, (d - 2) if arriving else (3 - d), zs]
            src = send_y.at[d - 2, zs]
        else:
            side = (d - 4) // 2
            dx = DIRS[d][0]
            out = pl.ds(4 if dx < 0 else 0, 4)
            into = pl.ds(4 if (dx > 0) == arriving else 0, 4)
            dst = recv_c.at[par, side if arriving else 1 - side, q, into, :]
            src = send_c.at[side, q, out, :]
        return remote(src, dst, ssem.at[d, q], sem, d)

    def pack(z, zi, slot):
        i = lax.rem(z, CH)
        packs = []
        for half in range(2):
            acc = zero
            for c in range(3):
                for xt in range(TILES):
                    v = eh[3 * half + c, zi, tile_rows(xt), :]
                    acc = jnp.where(
                        group == 5 * c + xt, lanes_roll(v, 40 * c + 8 * xt + 4), acc
                    )
            own_pack[half, slot] = acc
            packs.append(acc)
        pe, ph = packs
        down = jnp.where(low_half, lanes_roll(ph, -4), pe)
        up = jnp.where(low_half, pe, lanes_roll(ph, 4))
        here = (group == i) | (group == 5 + i) | (group == 10 + i)
        for side, v in ((0, down), (1, up)):
            send_y[side, slot] = v
            moved = jnp.where(sub < 4, lanes_roll(v, 8 * i + 96), lanes_roll(v, 8 * i))
            q = slot // CH
            send_c[side, q] = jnp.where(here, moved, send_c[side, q])

    def send(q, par):
        for d in range(8):
            start_if(d, message(d, q, par, False))

    xt0 = ((group == 0) | (group == 5) | (group == 10)) & (sub < 4)
    xt4 = ((group == 4) | (group == 9) | (group == 14)) & (sub >= 4)

    def unpack(z, zi, par, r):
        i = lax.rem(z, CH)
        q = z // CH
        packs = []
        for half in range(2):
            acc = own_pack[half, z]
            for c in range(3):
                v = recv_x[par, 3 * half + c, z]
                new = (e0, h0)[half]
                for xt in range(TILES):
                    old = eh[3 * half + c, z + PAD, tile_rows(xt), :]
                    if xt == 0:
                        old = jnp.where(sub < 4, v, old)
                    elif xt == 4:
                        old = jnp.where(sub < 4, old, v)
                    new[c, zi, tile_rows(xt), :] = old
                acc = jnp.where((group == 5 * c) & (sub < 4), lanes_roll(v, 40 * c + 4), acc)
                acc = jnp.where(
                    (group == 5 * c + 4) & (sub >= 4), lanes_roll(v, 40 * c + 36), acc
                )
            packs.append(acc)
        pe, ph = packs
        sides = []
        for side in range(2):
            v = recv_y[par, side, z]
            x = recv_c[par, side, q]
            v = jnp.where(xt0, lanes_roll(x, 128 - 8 * i), v)
            v = jnp.where(xt4, lanes_roll(x, 32 - 8 * i), v)
            sides.append(v)
        from_down, from_up = sides
        right = (
            jnp.where(low_half, pe, from_up),
            jnp.where(low_half, ph, lanes_roll(from_up, 4)),
        )
        left = (
            jnp.where(low_half, from_down, pe),
            jnp.where(low_half, lanes_roll(from_down, -4), ph),
        )
        for half in range(2):
            for c in range(3):
                strip0[3 * half + c, zi] = jnp.where(
                    lane < 64,
                    lanes_roll(right[half], -40 * c),
                    lanes_roll(left[half], 64 - 40 * c),
                )
        for c in range(2):
            a = lanes_roll(inject_a[z], 6 - 4 * c - r)
            b = lanes_roll(inject_b[z], 1 - 4 * c - r)
            strip_j[c, zi] = jnp.where(place == 6, a, jnp.where(place == 1, b, zero))

    loads[0].wait()
    loads[1].wait()

    def first_chunk(q, carry):
        for i in range(CH):
            pack(q * CH + i, q * CH + i + PAD, q * CH + i)
        send(q, 0)
        return carry

    lax.fori_loop(0, chunks, first_chunk, 0)

    loads[2].wait()

    def couple(z, carry):
        zi = z + PAD
        for xt in range(TILES):
            label = labels[zi, tile_rows(xt), :]
            value = zero
            for n in range(4):
                value = jnp.where(label == n, 0.5 * inverse[n], value)
            coup[zi, tile_rows(xt), :] = value
        return carry

    lax.fori_loop(0, nz, couple, 0)

    def c_copy(d, arriving):
        lower = (d == 0) == arriving
        src = coup.at[planes, pl.ds(TOP + 4 if d == 0 else TOP + 32, 4), :]
        dst = c_recv.at[:, pl.ds(0 if lower else 4, 4), :]
        return remote(src, dst, c_ssem.at[d], c_rsem.at[d if arriving else OPPOSITE[d]], d)

    for d in range(2):
        start_if(d, c_copy(d, False))

    total = w_send[...]
    for j in range(1, n_gx):
        w_copy(j, j, j).wait()
        total = total + w_all[j]
    loads[3].wait()
    for d in range(2):
        @pl.when(exists[d])
        def _():
            p_copy(d).wait_send()
            p_wait(d).wait_recv()
    parts = []
    for c in range(2):
        for g in range(4):
            keep = (lane < 32) & (lax.rem(lane // 4, 2) == c)
            parts.append(jnp.where(keep, lanes_roll(total, -32 * g), zero))
    weights = jnp.concatenate(parts, axis=0)
    first = start[0]
    last = start[0] + length[0]
    for xt in range(TILES):
        cells = pl.ds(8 * nz * xt, 8 * nz)
        now = lax.dot_general(
            profile[:, cells], weights, (((0,), (0,)), ((), ())),
            precision=HIGHEST, preferred_element_type=f32,
        )
        x = gx * 32 - 4 + 8 * xt + lax.broadcasted_iota(jnp.int32, (8 * nz, 128), 0) // nz
        j_flat[cells, :] = jnp.where((x >= first) & (x < last), now, 0.0)

    for d in range(2):
        wait_if(d, c_copy(d, True))
    where_at = offset[0]
    pick_row = lax.broadcasted_iota(jnp.int32, (128, 256), 0)
    pick_lane = lax.broadcasted_iota(jnp.int32, (128, 256), 1)
    pick_part = pick_row // 32
    pick_c = pick_lane // 128
    for t in range(TICKS):
        wanted = 8 * (t % K) + t // K + 4 * pick_c
        hit = (pick_row - 32 * pick_part == wanted) & (pick_row < 96)
        hit = hit & (pick_lane - 128 * pick_c == where_at)
        pick[t] = jnp.where(hit, 1.0, 0.0).astype(jnp.bfloat16)

    def prepare(z, carry):
        zi = z + PAD
        halo = c_recv[z]
        coup[zi, tile_rows(0), :] = jnp.where(sub < 4, halo, coup[zi, tile_rows(0), :])
        coup[zi, tile_rows(4), :] = jnp.where(sub < 4, coup[zi, tile_rows(4), :], halo)
        acc = zero
        j_parts = []
        for xt in range(TILES):
            v = coup[zi, tile_rows(xt), :]
            acc = jnp.where(group == xt, lanes_roll(v, 8 * xt + 4), acc)
            j = j_flat[pl.ds(z + 8 * nz * xt, 8, stride=nz), :]
            high = j.astype(jnp.bfloat16).astype(f32)
            middle = (j - high).astype(jnp.bfloat16).astype(f32)
            low = (j - high) - middle
            j_parts.append(
                jnp.where(lane < 32, high, 0.0)
                + jnp.where((lane >= 32) & (lane < 64), lanes_roll(middle, 32), 0.0)
                + jnp.where((lane >= 64) & (lane < 96), lanes_roll(low, 64), 0.0)
            )
            acc = jnp.where(group == 5 + xt, lanes_roll(j, 40 + 8 * xt), acc)
        j_all[zi] = jnp.concatenate([*j_parts, zero], axis=0).astype(jnp.bfloat16)
        v_send[0, z] = jnp.where((lane >= 40) & (where_at != 2), 0.0, acc)
        v_send[1, z] = jnp.where((lane >= 40) & (where_at != 125), 0.0, acc)
        return carry

    lax.fori_loop(0, nz, prepare, 0)

    def v_copy(d, arriving):
        return remote(
            v_send.at[d - 2], v_recv.at[(d - 2) if arriving else (3 - d)],
            v_ssem.at[d - 2], v_rsem.at[(d - 2) if arriving else (3 - d)], d,
        )

    for d in (2, 3):
        start_if(d, v_copy(d, False))
    for d in (2, 3):
        wait_if(d, v_copy(d, True))

    def finish(z, carry):
        zi = z + PAD
        own_down, own_up = v_send[0, z], v_send[1, z]
        from_down, from_up = v_recv[0, z], v_recv[1, z]
        right = jnp.where(low_half, own_up, from_up)
        left = jnp.where(low_half, from_down, own_up)
        strip_c[zi] = jnp.where(lane < 64, right, lanes_roll(left, 64))
        inject_a[z] = jnp.where(lane < 64, lanes_roll(from_up, -40), lanes_roll(own_down, 24))
        inject_b[z] = jnp.where(lane < 64, lanes_roll(own_up, -40), lanes_roll(from_down, 24))
        return carry

    lax.fori_loop(0, nz, finish, 0)
    loads[4].wait()

    outside_x = (sub < 4) & (gx == 0)
    half_first = jnp.where(outside_x, 0.0, jnp.full((8, 128), 0.5, f32))
    outside = (outside_x & ((group == 0) | (group == 8))) | (
        (lane >= 64) & low_half & (gy == 0)
    )
    half_strip = jnp.where(outside, 0.0, jnp.full((8, 128), 0.5, f32))

    def up_rows(v):
        return rows_roll(jnp.where(sub == 0, lanes_roll(v, -8), v), -1)

    def down_rows(v):
        return rows_roll(jnp.where(sub == 7, lanes_roll(v, 8), v), 1)

    def targets(s):
        if s == K - 1:
            return eh, eh, 3
        return e_at[s + 1], h_at[s + 1], 0

    def strip_step(zi, s):
        strip = strip_at[s]
        sx, sy, sz, tx, ty, tz = [strip[c, zi] for c in range(6)]
        sx_up, sy_up = strip[0, zi + 1], strip[1, zi + 1]
        sx_y, sz_y = lanes_roll(sx, -1), lanes_roll(sz, -1)
        sy_x, sz_x = up_rows(sy), up_rows(sz)
        ux = tx - half_strip * ((sz_y - sz) - (sy_up - sy))
        uy = ty - half_strip * ((sx_up - sx) - (sz_x - sz))
        uz = tz - half_strip * ((sy_x - sy) - (sx_y - sx))
        ghost_z = jnp.where(place == 4, sz, lanes_roll(ux, -62))
        ghost_x = jnp.where(place == 4, sx, lanes_roll(uz, -62))
        if s < K - 1:
            strip_new = strip_at[s + 1]
            tx_dn, ty_dn = strip_new[3, zi - 1], strip_new[4, zi - 1]
            c = strip_c[zi]
            vx = sx + c * ((uz - lanes_roll(uz, 1)) - (uy - ty_dn))
            vy = sy + c * ((ux - tx_dn) - (uz - down_rows(uz)))
            vz = sz + c * ((uy - down_rows(uy)) - (ux - lanes_roll(ux, 1)))
            if s == 0:
                vx = vx + strip_j[0, zi]
                vz = vz + strip_j[1, zi]
            for n, v in enumerate((vx, vy, vz, ux, uy, uz)):
                strip_new[n, zi] = v
        return [
            tuple(lanes_roll(g, 127 - (8 * xt + 4)) for g in (ghost_x, ghost_z))
            for xt in range(TILES)
        ]

    def magnetic_step(zi, s, ghosts):
        e_now, h_now = e_at[s], h_at[s]
        _, h_new, base = targets(s)
        for xt in range(TILES):
            rows = tile_rows(xt)
            above = pl.ds(TOP + 8 * xt + 1, 8)
            k = half_first if xt == 0 else 0.5
            ex, ey, ez = [e_now[n, zi, rows, :] for n in range(3)]
            hx, hy, hz = [h_now[n, zi, rows, :] for n in range(3)]
            ex_up, ey_up = e_now[0, zi + 1, rows, :], e_now[1, zi + 1, rows, :]
            ey_x, ez_x = e_now[1, zi, above, :], e_now[2, zi, above, :]
            ghost_x, ghost_z = ghosts[xt]
            ex_y = jnp.where(lane == 127, ghost_x, lanes_roll(ex, -1))
            ez_y = jnp.where(lane == 127, ghost_z, lanes_roll(ez, -1))
            h_new[base, zi, rows, :] = hx - k * ((ez_y - ez) - (ey_up - ey))
            h_new[base + 1, zi, rows, :] = hy - k * ((ex_up - ex) - (ez_x - ez))
            h_new[base + 2, zi, rows, :] = hz - k * ((ey_x - ey) - (ex_y - ex))

    def electric_step(zi, s, ghosts, sheet):
        e_now = e_at[s]
        e_new, h_new, base = targets(s)
        total = grads[s]
        around = []
        for xt in range(TILES):
            rows = tile_rows(xt)
            below = pl.ds(TOP + 8 * xt - 1, 8)
            around.append((
                [h_new[base + n, zi, rows, :] for n in range(3)],
                [h_new[base + n, zi - 1, rows, :] for n in range(2)],
                [h_new[base + n, zi, below, :] for n in range(1, 3)],
            ))
        for xt in range(TILES):
            rows = tile_rows(xt)
            (hx, hy, hz), (hx_dn, hy_dn), (hy_x, hz_x) = around[xt]
            ex, ey, ez = [e_now[n, zi, rows, :] for n in range(3)]
            ghost_z, ghost_x = ghosts[xt]
            hx_y = jnp.where(lane == 0, ghost_x, lanes_roll(hx, 1))
            hz_y = jnp.where(lane == 0, ghost_z, lanes_roll(hz, 1))
            cc = coup[zi, rows, :]
            at = slice(8 * xt, 8 * xt + 8)
            ex = ex + cc * ((hz - hz_y) - (hy - hy_dn)) + sheet[at, :128]
            ey = ey + cc * ((hx - hx_dn) - (hz - hz_x))
            ez = ez + cc * ((hy - hy_x) - (hx - hx_y)) + sheet[at, 128:]
            e_new[0, zi, rows, :] = ex
            e_new[1, zi, rows, :] = ey
            e_new[2, zi, rows, :] = ez
            total[zi, rows, :] = total[zi, rows, :] + (
                ex * fwd[0, zi, rows, :] + ey * fwd[1, zi, rows, :] + ez * fwd[2, zi, rows, :]
            )

    def stores(q):
        z0 = pl.multiple_of(q * CH, CH)
        zs = pl.ds(z0 + PAD, CH)
        out = pl.ds(z0, CH)
        return (
            pltpu.make_async_copy(
                eh.at[pl.ds(0, 3), zs, own_rows, :], e_out.at[:, out], out_sem.at[0, q]
            ),
            pltpu.make_async_copy(
                eh.at[pl.ds(3, 3), zs, own_rows, :], h_out.at[:, out], out_sem.at[1, q]
            ),
            pltpu.make_async_copy(
                grad0.at[zs, own_rows, :], g_out.at[out], out_sem.at[2, q]
            ),
        )

    cells = ROUNDS * nz

    def spot(at):
        valid = jnp.logical_and(at >= 0, at < cells)
        at = jnp.clip(at, 0, cells - 1)
        z = lax.rem(at, nz)
        return valid, at // nz, z, jnp.where(valid, z + PAD, nz + PAD + 2)

    def wave(w):
        valid, _, z, zi = spot(w - 9)
        pack(z, zi, jnp.where(valid, z, nz))
        order = tuple(reversed(range(K)))
        spots = {s: spot(w - 2 - 2 * s) for s in order}
        sheets = {}
        ghosts = {}
        for s in order:
            _, r, _, zi = spots[s]
            sheets[s] = jnp.dot(j_all[zi], pick[r * K + s], preferred_element_type=f32)
            ghosts[s] = strip_step(zi, s)
        for s in order:
            magnetic_step(spots[s][3], s, ghosts[s])
        for s in order:
            electric_step(spots[s][3], s, ghosts[s], sheets[s])
        valid, r, z, zi = spot(w)
        unpack(z, zi, lax.rem(r, 2), r)

    def one_chunk(n, carry):
        r = n // chunks
        q = n - r * chunks

        @pl.when(r < ROUNDS)
        def _():
            for d in range(8):
                wait_if(d, message(d, q, lax.rem(r, 2), True))

        def waves(i, carry):
            wave(n * CH + i)

            @pl.when(i == 0)
            def _():
                done = n - 3
                done_r = (done + chunks) // chunks
                done_q = lax.rem(done + chunks, chunks)

                @pl.when(jnp.logical_and(done >= 0, done_r < ROUNDS))
                def _():
                    send(done_q, lax.rem(done_r, 2))

                @pl.when(done_r == ROUNDS)
                def _():
                    for j in range(CH):
                        zi = done_q * CH + j + PAD
                        for xt in range(TILES):
                            rows = tile_rows(xt)
                            grad0[zi, rows, :] = (grad0[zi, rows, :] + grad1[zi, rows, :]) + (
                                grad2[zi, rows, :] + grad3[zi, rows, :]
                            )
                    for store in stores(done_q):
                        store.start()

            return carry

        return lax.fori_loop(0, CH, waves, carry)

    lax.fori_loop(0, ROUNDS * chunks + 3, one_chunk, 0)

    def finish_stores(q, carry):
        for store in stores(q):
            store.wait()
        return carry

    lax.fori_loop(0, chunks, finish_stores, 0)


def shards(n_gx, n_gy, *args):
    (electric, magnetic, forward_field, material, inv_permittivity, spectral_rate,
     intersection_partial, mode_profile, sheet_offset, plane_start, monitor_length) = args
    nz = electric.shape[1]
    f32 = jnp.float32
    zp = nz + PAD + EXTRA
    chunks = nz // CH
    dma = pltpu.SemaphoreType.DMA
    vmem = lambda *shape: pltpu.VMEM(shape, f32)
    anyspace = pl.BlockSpec(memory_space=pl.ANY)
    smem = pl.BlockSpec(memory_space=pltpu.SMEM)
    vm = pl.BlockSpec(memory_space=pltpu.VMEM)
    e, h, g = pl.pallas_call(
        functools.partial(kernel, n_gx, n_gy, nz),
        out_shape=[
            jax.ShapeDtypeStruct(electric.shape, f32),
            jax.ShapeDtypeStruct(electric.shape, f32),
            jax.ShapeDtypeStruct(material.shape, f32),
        ],
        in_specs=[anyspace, anyspace, anyspace, anyspace, smem, vm, vm, anyspace, smem, smem, smem],
        out_specs=[anyspace] * 3,
        scratch_shapes=[
            vmem(6, zp, ROWS, 128),
            *[vmem(3, zp, ROWS, 128) for _ in range(2 * K)],
            *[vmem(6, zp, 8, 128) for _ in range(K)],
            *[vmem(zp, ROWS, 128) for _ in range(K)],
            vmem(zp, ROWS, 128),
            vmem(3, zp, ROWS, 128),
            pltpu.VMEM((zp, ROWS, 128), jnp.int32),
            vmem(zp, 8, 128),
            vmem(2, zp, 8, 128),
            vmem(2, nz + CH, 8, 128),
            vmem(2, nz + CH, 8, 128),
            vmem(2, chunks + 1, 8, 128),
            vmem(2, 6, nz, 8, 128),
            vmem(2, 2, nz, 8, 128),
            vmem(2, 2, chunks, 8, 128),
            vmem(8, 128),
            vmem(n_gx, 8, 128),
            vmem(64, 40 * nz),
            vmem(40 * nz, 128),
            pltpu.VMEM((zp, 48, 128), jnp.bfloat16),
            pltpu.VMEM((TICKS, 128, 256), jnp.bfloat16),
            vmem(2, nz, 8, 128),
            vmem(2, nz, 8, 128),
            vmem(nz, 8, 128),
            vmem(nz, 8, 128),
            vmem(nz, 8, 128),
            dma((6,)),
            dma((3, chunks)),
            dma((8, chunks)),
            dma((2, 8, chunks)),
            dma((n_gx,)),
            dma((n_gx,)),
            dma((2,)),
            dma((2,)),
            dma((2,)),
            dma((2,)),
            dma((2,)),
            dma((2,)),
        ],
        compiler_params=pltpu.CompilerParams(
            collective_id=0, has_side_effects=True, vmem_limit_bytes=56 << 20
        ),
    )(
        electric, magnetic, forward_field, material, inv_permittivity,
        spectral_rate.reshape(1, -1), intersection_partial,
        mode_profile.reshape(-1, mode_profile.shape[2]),
        sheet_offset, plane_start, monitor_length,
    )
    return e, h, g * (1.0 / TICKS)


def solution(mesh):
    placed = (
        P(None, None, "gx", "gy"),
        P(None, None, "gx", "gy"),
        P(None, None, "gx", "gy"),
        P(None, "gx", "gy"),
        P(),
        P(),
        P("gx", "gy", None),
        P("gy", None, "gx"),
        P("gy"),
        P("gy"),
        P("gy"),
    )
    return jax.shard_map(
        functools.partial(shards, mesh.shape["gx"], mesh.shape["gy"]),
        mesh=mesh,
        in_specs=placed,
        out_specs=(P(None, None, "gx", "gy"), P(None, None, "gx", "gy"), P(None, "gx", "gy")),
        check_vma=False,
    )
```

time: 233 us -> 137 us (0.59)
  the two profiles are of different devices: /device:TPU:33 before, /device:TPU:163 now
where the time goes in v2:
time: 137 us
  Pallas kernels  128 us (93%)
  local copies, waits for them, and re-layouts  3.93 us (3%)
  between operations  2.58 us (2%)
  other arithmetic  1.88 us (1%)
    pallas_call x1, Pallas kernels, shards(): pl.pallas_call(functools.partial(kernel, n_gx, n_gy, nz), out_shape=[jax....  128 us
    unnamed x4, local copies, waits for them, and re-layouts  3.93 us

profile of v2, /device:TPU:163, one launch (start us, length us, event | category | flops | bytes accessed | tf_op | source)
XLA Modules:
  0.0 136.8 jit_solution(9470664691491235501)
XLA Ops:
  2.6 128.4 %shard_map.130 = (f32[3,32,32,128]{3,2,1,0:T(8,128)}, f32[3,32,32,128]{3,2,1,0:T(8,128)}, f32[32,32,128]{2,1,0:T(8,128)}) custom-call(f32[3,32,32,128]{3,2,1,0:T(8,128)} %e_in.1, f32[3,32,32,128]{3,2,1,0:T(8,128)} %h_in.1, f32[3,32,32,128]{3,2,1,0:T(8,128)} %f_in.1, s32[32,32,128]{2,1,0:T(8,128)} %material_in.1, f32[4]{0:T(128)} %inverse.1, ...), custom_call_target="tpu_custom_call" | custom-call | tf_op jit(solution)/shard_map/pallas_call | solution.py:644
  131.0 1.9 %broadcast_multiply_fusion = f32[32,32,128]{2,1,0:T(8,128)} fusion(f32[32,32,128]{2,1,0:T(8,128)} %get-tuple-element.8), kind=kLoop, calls=%fused_computation | loop fusion | flops 131072 | bytes 1048576 | tf_op jit(solution)/shard_map/mul | solution.py:702
  132.9 0.0 copy-start
  132.9 2.8 %copy.19 = f32[3,32,32,128]{3,2,1,0:T(8,128)} copy(f32[3,32,32,128]{3,2,1,0:T(8,128)} %get-tuple-element.12) | data formatting | bytes 3145728
  135.6 0.0 copy-done
  135.6 1.1 copy.20
Async XLA Ops:
  132.9 2.8 %copy-start = (f32[3,32,32,128]{3,2,1,0:T(8,128)S(1)}, f32[3,32,32,128]{3,2,1,0:T(8,128)}, u32[]{:S(2)}) copy-start(f32[3,32,32,128]{3,2,1,0:T(8,128)} %get-tuple-element.13) | copy-start | bytes 4718596

commit v3 on v2

--- a/solution.py
+++ b/solution.py
@@ -12,6 +12,7 @@
 K = 4
 ROUNDS = TICKS // K
 CH = 4
+BLOCK = 8
 TILES = 5
 TOP = 8
 ROWS = 56
@@ -43,12 +44,13 @@
     e_in, h_in, f_in, material_in, inverse, rate, partial, profile_in, offset, start, length,
     e_out, h_out, g_out,
     eh, e0, h0, e1, h1, e2, h2, e3, h3, strip0, strip1, strip2, strip3,
-    grad0, grad1, grad2, grad3, coup, fwd, labels, strip_c, strip_j, own_pack,
+    grad0, grad1, grad2, grad3, coup, fwd, labels, strip_c, strip_j, ghost, own_pack,
     send_y, send_c, recv_x, recv_y, recv_c,
     w_send, w_all, profile, j_flat, j_all, pick, v_send, v_recv, c_recv, inject_a, inject_b,
     load_sem, out_sem, ssem, rsem, w_ssem, w_rsem, p_ssem, p_rsem, c_ssem, c_rsem, v_ssem, v_rsem,
 ):
     chunks = nz // CH
+    blocks = nz // BLOCK
     gx = lax.axis_index("gx")
     gy = lax.axis_index("gy")
     f32 = jnp.float32
@@ -71,6 +73,14 @@
         exists.append(ok)
         devices.append((gx + dx, gy + dy))
 
+    barrier = pltpu.get_barrier_semaphore()
+    for j in range(1, n_gx):
+        peer = (lax.rem(gx + j, n_gx), gy)
+        pl.semaphore_signal(barrier, inc=1, device_id=peer, device_id_type=MESH)
+    for d in range(2, 8):
+        @pl.when(exists[d])
+        def _():
+            pl.semaphore_signal(barrier, inc=1, device_id=devices[d], device_id_type=MESH)
     e_at = (e0, e1, e2, e3)
     h_at = (h0, h1, h2, h3, eh)
     strip_at = (strip0, strip1, strip2, strip3)
@@ -104,7 +114,7 @@
                 total[zi, tile_rows(xt), :] = zero
         return carry
 
-    lax.fori_loop(PAD, nz + PAD, clear, 0)
+    lax.fori_loop(PAD, nz + PAD, clear, 0, unroll=4)
 
     def clear_x(side):
         rows = pl.ds(4 * side, 4)
@@ -147,35 +157,6 @@
             for par in range(2):
                 for q in range(chunks):
                     recv_c[par, (d - 4) // 2, q, rows, :] = jnp.zeros((4, 128), f32)
-
-    barrier = pltpu.get_barrier_semaphore()
-    for j in range(1, n_gx):
-        peer = (lax.rem(gx + j, n_gx), gy)
-        pl.semaphore_signal(barrier, inc=1, device_id=peer, device_id_type=MESH)
-    for d in range(2, 8):
-        @pl.when(exists[d])
-        def _():
-            pl.semaphore_signal(barrier, inc=1, device_id=devices[d], device_id_type=MESH)
-    one = lambda flag: jnp.where(flag, 1, 0)
-    near_x = one(exists[0]) + one(exists[1])
-    near_y = one(exists[2]) + one(exists[3])
-    pl.semaphore_wait(barrier, n_gx - 1 + near_y * (1 + near_x))
-
-    def remote(src, dst, send, recv, d):
-        return pltpu.make_async_remote_copy(
-            src_ref=src, dst_ref=dst, send_sem=send, recv_sem=recv,
-            device_id=devices[d], device_id_type=MESH,
-        )
-
-    def start_if(d, copy):
-        @pl.when(exists[d])
-        def _():
-            copy.start()
-
-    def wait_if(d, copy):
-        @pl.when(exists[d])
-        def _():
-            copy.wait()
 
     row = lax.broadcasted_iota(jnp.int32, (32, 128), 0)
     tick = (4 * (row - (row // 4) * 4) + row // 8).astype(f32)
@@ -194,6 +175,36 @@
         packed = jnp.where(lane // 32 == g, term[8 * g : 8 * g + 8], packed)
     w_send[...] = packed
 
+    def remote(src, dst, send, recv, d):
+        return pltpu.make_async_remote_copy(
+            src_ref=src, dst_ref=dst, send_sem=send, recv_sem=recv,
+            device_id=devices[d], device_id_type=MESH,
+        )
+
+    def start_if(d, copy):
+        @pl.when(exists[d])
+        def _():
+            copy.start()
+
+    def wait_if(d, copy):
+        @pl.when(exists[d])
+        def _():
+            copy.wait()
+
+    loads[2].wait()
+
+    def couple(z, carry):
+        zi = z + PAD
+        for xt in range(TILES):
+            label = labels[zi, tile_rows(xt), :]
+            value = zero
+            for n in range(4):
+                value = jnp.where(label == n, 0.5 * inverse[n], value)
+            coup[zi, tile_rows(xt), :] = value
+        return carry
+
+    lax.fori_loop(0, nz, couple, 0, unroll=4)
+
     def w_copy(j, slot, sem_slot):
         peer = (lax.rem(gx + j, n_gx), gy)
         return pltpu.make_async_remote_copy(
@@ -201,6 +212,11 @@
             recv_sem=w_rsem.at[sem_slot], device_id=peer, device_id_type=MESH,
         )
 
+    one = lambda flag: jnp.where(flag, 1, 0)
+    near_x = one(exists[0]) + one(exists[1])
+    near_y = one(exists[2]) + one(exists[3])
+    pl.semaphore_wait(barrier, n_gx - 1 + near_y * (1 + near_x))
+
     for j in range(1, n_gx):
         w_copy(j, j, j).start()
 
@@ -217,14 +233,23 @@
     for d in range(2):
         start_if(d, p_copy(d))
 
+    def c_copy(d, arriving):
+        lower = (d == 0) == arriving
+        src = coup.at[planes, pl.ds(TOP + 4 if d == 0 else TOP + 32, 4), :]
+        dst = c_recv.at[:, pl.ds(0 if lower else 4, 4), :]
+        return remote(src, dst, c_ssem.at[d], c_rsem.at[d if arriving else OPPOSITE[d]], d)
+
+    for d in range(2):
+        start_if(d, c_copy(d, False))
+
     def message(d, q, par, arriving):
-        z0 = pl.multiple_of(q * CH, CH)
-        zs = pl.ds(z0, CH)
+        z0 = pl.multiple_of(q * BLOCK, BLOCK)
+        zs = pl.ds(z0, BLOCK)
         sem = rsem.at[par, d if arriving else OPPOSITE[d], q]
         if d < 2:
             lower = (d == 0) == arriving
             dst = recv_x.at[par, :, zs, pl.ds(0 if lower else 4, 4), :]
-            src = eh.at[:, pl.ds(z0 + PAD, CH), pl.ds(TOP + 4 if d == 0 else TOP + 32, 4), :]
+            src = eh.at[:, pl.ds(z0 + PAD, BLOCK), pl.ds(TOP + 4 if d == 0 else TOP + 32, 4), :]
         elif d < 4:
             dst = recv_y.at[par, (d - 2) if arriving else (3 - d), zs]
             src = send_y.at[d - 2, zs]
@@ -233,24 +258,22 @@
             dx = DIRS[d][0]
             out = pl.ds(4 if dx < 0 else 0, 4)
             into = pl.ds(4 if (dx > 0) == arriving else 0, 4)
-            dst = recv_c.at[par, side if arriving else 1 - side, q, into, :]
-            src = send_c.at[side, q, out, :]
+            corners = pl.ds(q * (BLOCK // CH), BLOCK // CH)
+            dst = recv_c.at[par, side if arriving else 1 - side, corners, into, :]
+            src = send_c.at[side, corners, out, :]
         return remote(src, dst, ssem.at[d, q], sem, d)
 
-    def pack(z, zi, slot):
+    def pack_half(zi, slot, half):
+        acc = zero
+        for c in range(3):
+            for xt in range(TILES):
+                v = eh[3 * half + c, zi, tile_rows(xt), :]
+                acc = jnp.where(group == 5 * c + xt, lanes_roll(v, 40 * c + 8 * xt + 4), acc)
+        own_pack[half, slot] = acc
+        return acc
+
+    def pack_sides(z, slot, pe, ph):
         i = lax.rem(z, CH)
-        packs = []
-        for half in range(2):
-            acc = zero
-            for c in range(3):
-                for xt in range(TILES):
-                    v = eh[3 * half + c, zi, tile_rows(xt), :]
-                    acc = jnp.where(
-                        group == 5 * c + xt, lanes_roll(v, 40 * c + 8 * xt + 4), acc
-                    )
-            own_pack[half, slot] = acc
-            packs.append(acc)
-        pe, ph = packs
         down = jnp.where(low_half, lanes_roll(ph, -4), pe)
         up = jnp.where(low_half, pe, lanes_roll(ph, 4))
         here = (group == i) | (group == 5 + i) | (group == 10 + i)
@@ -260,6 +283,9 @@
             q = slot // CH
             send_c[side, q] = jnp.where(here, moved, send_c[side, q])
 
+    def pack(z, zi, slot):
+        pack_sides(z, slot, pack_half(zi, slot, 0), pack_half(zi, slot, 1))
+
     def send(q, par):
         for d in range(8):
             start_if(d, message(d, q, par, False))
@@ -267,15 +293,11 @@
     xt0 = ((group == 0) | (group == 5) | (group == 10)) & (sub < 4)
     xt4 = ((group == 4) | (group == 9) | (group == 14)) & (sub >= 4)
 
-    def unpack(z, zi, par, r):
-        i = lax.rem(z, CH)
-        q = z // CH
-        packs = []
+    def unpack_tiles(z, zi, par):
         for half in range(2):
-            acc = own_pack[half, z]
+            new = (e0, h0)[half]
             for c in range(3):
                 v = recv_x[par, 3 * half + c, z]
-                new = (e0, h0)[half]
                 for xt in range(TILES):
                     old = eh[3 * half + c, z + PAD, tile_rows(xt), :]
                     if xt == 0:
@@ -283,11 +305,18 @@
                     elif xt == 4:
                         old = jnp.where(sub < 4, old, v)
                     new[c, zi, tile_rows(xt), :] = old
-                acc = jnp.where((group == 5 * c) & (sub < 4), lanes_roll(v, 40 * c + 4), acc)
-                acc = jnp.where(
-                    (group == 5 * c + 4) & (sub >= 4), lanes_roll(v, 40 * c + 36), acc
-                )
-            packs.append(acc)
+
+    def unpack_strips(z, zi, par, r):
+        i = lax.rem(z, CH)
+        q = z // CH
+        packs = []
+        for half in range(2):
+            edge = zero
+            for c in range(3):
+                v = recv_x[par, 3 * half + c, z]
+                edge = jnp.where(group == 5 * c, lanes_roll(v, 40 * c + 4), edge)
+            acc = jnp.where(xt0, edge, own_pack[half, z])
+            packs.append(jnp.where(xt4, lanes_roll(edge, 32), acc))
         pe, ph = packs
         sides = []
         for side in range(2):
@@ -320,36 +349,22 @@
     loads[0].wait()
     loads[1].wait()
 
-    def first_chunk(q, carry):
-        for i in range(CH):
-            pack(q * CH + i, q * CH + i + PAD, q * CH + i)
-        send(q, 0)
+    def first_block(q, carry):
+        def first(i, carry):
+            for j in range(CH):
+                z = q * BLOCK + i * CH + j
+                pack(z, z + PAD, z)
+            return carry
+
+        lax.fori_loop(0, BLOCK // CH, first, 0)
+
+        @pl.when(q < blocks // 2)
+        def _():
+            send(q, 0)
+
         return carry
 
-    lax.fori_loop(0, chunks, first_chunk, 0)
-
-    loads[2].wait()
-
-    def couple(z, carry):
-        zi = z + PAD
-        for xt in range(TILES):
-            label = labels[zi, tile_rows(xt), :]
-            value = zero
-            for n in range(4):
-                value = jnp.where(label == n, 0.5 * inverse[n], value)
-            coup[zi, tile_rows(xt), :] = value
-        return carry
-
-    lax.fori_loop(0, nz, couple, 0)
-
-    def c_copy(d, arriving):
-        lower = (d == 0) == arriving
-        src = coup.at[planes, pl.ds(TOP + 4 if d == 0 else TOP + 32, 4), :]
-        dst = c_recv.at[:, pl.ds(0 if lower else 4, 4), :]
-        return remote(src, dst, c_ssem.at[d], c_rsem.at[d if arriving else OPPOSITE[d]], d)
-
-    for d in range(2):
-        start_if(d, c_copy(d, False))
+    lax.fori_loop(0, blocks, first_block, 0)
 
     total = w_send[...]
     for j in range(1, n_gx):
@@ -381,6 +396,62 @@
     for d in range(2):
         wait_if(d, c_copy(d, True))
     where_at = offset[0]
+    def prepare(z, carry):
+        zi = z + PAD
+        halo = c_recv[z]
+        acc = zero
+        for xt in range(TILES):
+            v = coup[zi, tile_rows(xt), :]
+            if xt == 0:
+                v = jnp.where(sub < 4, halo, v)
+                coup[zi, tile_rows(xt), :] = v
+            elif xt == 4:
+                v = jnp.where(sub < 4, v, halo)
+                coup[zi, tile_rows(xt), :] = v
+            acc = jnp.where(group == xt, lanes_roll(v, 8 * xt + 4), acc)
+            j = j_flat[pl.ds(z + 8 * nz * xt, 8, stride=nz), :]
+            acc = jnp.where(group == 5 + xt, lanes_roll(j, 40 + 8 * xt), acc)
+        v_send[0, z] = jnp.where((lane >= 40) & (where_at != 2), 0.0, acc)
+        v_send[1, z] = jnp.where((lane >= 40) & (where_at != 125), 0.0, acc)
+        return carry
+
+    def v_copy(d, q, arriving):
+        zs = pl.ds(pl.multiple_of(q * BLOCK, BLOCK), BLOCK)
+        side = (d - 2) if arriving else (3 - d)
+        return remote(
+            v_send.at[d - 2, zs], v_recv.at[side, zs], v_ssem.at[d - 2, q], v_rsem.at[side, q], d
+        )
+
+    def prepare_block(q, carry):
+        lax.fori_loop(0, BLOCK, lambda j, c: prepare(q * BLOCK + j, c), 0, unroll=4)
+        for d in (2, 3):
+            start_if(d, v_copy(d, q, False))
+        return carry
+
+    lax.fori_loop(0, blocks, prepare_block, 0)
+
+    def later_block(q, carry):
+        send(q, 0)
+        return carry
+
+    lax.fori_loop(blocks // 2, blocks, later_block, 0)
+
+    def split(z, carry):
+        j_parts = []
+        for xt in range(TILES):
+            j = j_flat[pl.ds(z + 8 * nz * xt, 8, stride=nz), :]
+            high = j.astype(jnp.bfloat16).astype(f32)
+            middle = (j - high).astype(jnp.bfloat16).astype(f32)
+            low = (j - high) - middle
+            j_parts.append(
+                jnp.where(lane < 32, high, 0.0)
+                + jnp.where((lane >= 32) & (lane < 64), lanes_roll(middle, 32), 0.0)
+                + jnp.where((lane >= 64) & (lane < 96), lanes_roll(low, 64), 0.0)
+            )
+        j_all[z + PAD] = jnp.concatenate([*j_parts, zero], axis=0).astype(jnp.bfloat16)
+        return carry
+
+    lax.fori_loop(0, nz, split, 0, unroll=4)
     pick_row = lax.broadcasted_iota(jnp.int32, (128, 256), 0)
     pick_lane = lax.broadcasted_iota(jnp.int32, (128, 256), 1)
     pick_part = pick_row // 32
@@ -390,44 +461,6 @@
         hit = (pick_row - 32 * pick_part == wanted) & (pick_row < 96)
         hit = hit & (pick_lane - 128 * pick_c == where_at)
         pick[t] = jnp.where(hit, 1.0, 0.0).astype(jnp.bfloat16)
-
-    def prepare(z, carry):
-        zi = z + PAD
-        halo = c_recv[z]
-        coup[zi, tile_rows(0), :] = jnp.where(sub < 4, halo, coup[zi, tile_rows(0), :])
-        coup[zi, tile_rows(4), :] = jnp.where(sub < 4, coup[zi, tile_rows(4), :], halo)
-        acc = zero
-        j_parts = []
-        for xt in range(TILES):
-            v = coup[zi, tile_rows(xt), :]
-            acc = jnp.where(group == xt, lanes_roll(v, 8 * xt + 4), acc)
-            j = j_flat[pl.ds(z + 8 * nz * xt, 8, stride=nz), :]
-            high = j.astype(jnp.bfloat16).astype(f32)
-            middle = (j - high).astype(jnp.bfloat16).astype(f32)
-            low = (j - high) - middle
-            j_parts.append(
-                jnp.where(lane < 32, high, 0.0)
-                + jnp.where((lane >= 32) & (lane < 64), lanes_roll(middle, 32), 0.0)
-                + jnp.where((lane >= 64) & (lane < 96), lanes_roll(low, 64), 0.0)
-            )
-            acc = jnp.where(group == 5 + xt, lanes_roll(j, 40 + 8 * xt), acc)
-        j_all[zi] = jnp.concatenate([*j_parts, zero], axis=0).astype(jnp.bfloat16)
-        v_send[0, z] = jnp.where((lane >= 40) & (where_at != 2), 0.0, acc)
-        v_send[1, z] = jnp.where((lane >= 40) & (where_at != 125), 0.0, acc)
-        return carry
-
-    lax.fori_loop(0, nz, prepare, 0)
-
-    def v_copy(d, arriving):
-        return remote(
-            v_send.at[d - 2], v_recv.at[(d - 2) if arriving else (3 - d)],
-            v_ssem.at[d - 2], v_rsem.at[(d - 2) if arriving else (3 - d)], d,
-        )
-
-    for d in (2, 3):
-        start_if(d, v_copy(d, False))
-    for d in (2, 3):
-        wait_if(d, v_copy(d, True))
 
     def finish(z, carry):
         zi = z + PAD
@@ -440,7 +473,6 @@
         inject_b[z] = jnp.where(lane < 64, lanes_roll(own_up, -40), lanes_roll(from_down, 24))
         return carry
 
-    lax.fori_loop(0, nz, finish, 0)
     loads[4].wait()
 
     outside_x = (sub < 4) & (gx == 0)
@@ -484,10 +516,9 @@
                 vz = vz + strip_j[1, zi]
             for n, v in enumerate((vx, vy, vz, ux, uy, uz)):
                 strip_new[n, zi] = v
-        return [
-            tuple(lanes_roll(g, 127 - (8 * xt + 4)) for g in (ghost_x, ghost_z))
-            for xt in range(TILES)
-        ]
+        for xt in range(TILES):
+            ghost[s, xt, 0] = lanes_roll(ghost_x, 127 - (8 * xt + 4))
+            ghost[s, xt, 1] = lanes_roll(ghost_z, 127 - (8 * xt + 4))
 
     def magnetic_step(zi, s, ghosts):
         e_now, h_now = e_at[s], h_at[s]
@@ -540,9 +571,9 @@
             )
 
     def stores(q):
-        z0 = pl.multiple_of(q * CH, CH)
-        zs = pl.ds(z0 + PAD, CH)
-        out = pl.ds(z0, CH)
+        z0 = pl.multiple_of(q * BLOCK, BLOCK)
+        zs = pl.ds(z0 + PAD, BLOCK)
+        out = pl.ds(z0, BLOCK)
         return (
             pltpu.make_async_copy(
                 eh.at[pl.ds(0, 3), zs, own_rows, :], e_out.at[:, out], out_sem.at[0, q]
@@ -564,40 +595,63 @@
         return valid, at // nz, z, jnp.where(valid, z + PAD, nz + PAD + 2)
 
     def wave(w):
-        valid, _, z, zi = spot(w - 9)
-        pack(z, zi, jnp.where(valid, z, nz))
-        order = tuple(reversed(range(K)))
-        spots = {s: spot(w - 2 - 2 * s) for s in order}
-        sheets = {}
-        ghosts = {}
-        for s in order:
-            _, r, _, zi = spots[s]
-            sheets[s] = jnp.dot(j_all[zi], pick[r * K + s], preferred_element_type=f32)
-            ghosts[s] = strip_step(zi, s)
-        for s in order:
-            magnetic_step(spots[s][3], s, ghosts[s])
-        for s in order:
-            electric_step(spots[s][3], s, ghosts[s], sheets[s])
-        valid, r, z, zi = spot(w)
-        unpack(z, zi, lax.rem(r, 2), r)
-
-    def one_chunk(n, carry):
-        r = n // chunks
-        q = n - r * chunks
+        spots = {s: spot(w - 3 - 2 * s) for s in range(K)}
+        held = {}
+        sheet = {}
+        p_valid, _, p_z, p_zi = spot(w - 10)
+        p_slot = jnp.where(p_valid, p_z, nz)
+        _, u_r, u_z, u_zi = spot(w)
+        held[0] = [(ghost[0, xt, 0], ghost[0, xt, 1]) for xt in range(TILES)]
+        held[3] = [(ghost[3, xt, 0], ghost[3, xt, 1]) for xt in range(TILES)]
+        strip_step(spot(w - 2 - 2 * 3)[3], 3)
+        held[1] = [(ghost[1, xt, 0], ghost[1, xt, 1]) for xt in range(TILES)]
+        held[2] = [(ghost[2, xt, 0], ghost[2, xt, 1]) for xt in range(TILES)]
+        strip_step(spot(w - 2 - 2 * 2)[3], 2)
+        sheet[1] = jnp.dot(j_all[spots[1][3]], pick[spots[1][1] * K + 1], preferred_element_type=f32)
+        strip_step(spot(w - 2 - 2 * 1)[3], 1)
+        strip_step(spot(w - 2 - 2 * 0)[3], 0)
+        half0 = pack_half(p_zi, p_slot, 0)
+        magnetic_step(spots[3][3], 3, held[3])
+        half1 = pack_half(p_zi, p_slot, 1)
+        magnetic_step(spots[2][3], 2, held[2])
+        magnetic_step(spots[1][3], 1, held[1])
+        magnetic_step(spots[0][3], 0, held[0])
+        electric_step(spots[1][3], 1, held[1], sheet[1])
+        sheet[2] = jnp.dot(j_all[spots[2][3]], pick[spots[2][1] * K + 2], preferred_element_type=f32)
+        sheet[0] = jnp.dot(j_all[spots[0][3]], pick[spots[0][1] * K + 0], preferred_element_type=f32)
+        sheet[3] = jnp.dot(j_all[spots[3][3]], pick[spots[3][1] * K + 3], preferred_element_type=f32)
+        electric_step(spots[0][3], 0, held[0], sheet[0])
+        pack_sides(p_z, p_slot, half0, half1)
+        electric_step(spots[2][3], 2, held[2], sheet[2])
+        electric_step(spots[3][3], 3, held[3], sheet[3])
+        unpack_strips(u_z, u_zi, lax.rem(u_r, 2), u_r)
+        unpack_tiles(u_z, u_zi, lax.rem(u_r, 2))
+
+    last_wave = cells + 10
+
+    def one_block(n, carry):
+        r = n // blocks
+        q = n - r * blocks
 
         @pl.when(r < ROUNDS)
         def _():
             for d in range(8):
                 wait_if(d, message(d, q, lax.rem(r, 2), True))
 
+        @pl.when(n < blocks)
+        def _():
+            for d in (2, 3):
+                wait_if(d, v_copy(d, n, True))
+            lax.fori_loop(0, BLOCK, lambda j, c: finish(n * BLOCK + j, c), 0, unroll=4)
+
         def waves(i, carry):
-            wave(n * CH + i)
-
-            @pl.when(i == 0)
+            wave(n * BLOCK + i)
+
+            @pl.when(i == 1)
             def _():
-                done = n - 3
-                done_r = (done + chunks) // chunks
-                done_q = lax.rem(done + chunks, chunks)
+                done = n - 2
+                done_r = (done + blocks) // blocks
+                done_q = lax.rem(done + blocks, blocks)
 
                 @pl.when(jnp.logical_and(done >= 0, done_r < ROUNDS))
                 def _():
@@ -605,28 +659,51 @@
 
                 @pl.when(done_r == ROUNDS)
                 def _():
-                    for j in range(CH):
-                        zi = done_q * CH + j + PAD
+                    def add(j, carry):
+                        zi = done_q * BLOCK + j + PAD
                         for xt in range(TILES):
                             rows = tile_rows(xt)
-                            grad0[zi, rows, :] = (grad0[zi, rows, :] + grad1[zi, rows, :]) + (
+                            total = (grad0[zi, rows, :] + grad1[zi, rows, :]) + (
                                 grad2[zi, rows, :] + grad3[zi, rows, :]
                             )
+                            grad0[zi, rows, :] = total * (1.0 / TICKS)
+                        return carry
+
+                    lax.fori_loop(0, BLOCK, add, 0, unroll=4)
                     for store in stores(done_q):
                         store.start()
 
             return carry
 
-        return lax.fori_loop(0, CH, waves, carry)
-
-    lax.fori_loop(0, ROUNDS * chunks + 3, one_chunk, 0)
+        return lax.fori_loop(0, jnp.minimum(BLOCK, last_wave - n * BLOCK), waves, carry)
+
+    lax.fori_loop(0, (last_wave + BLOCK - 1) // BLOCK, one_block, 0)
 
     def finish_stores(q, carry):
         for store in stores(q):
             store.wait()
         return carry
 
-    lax.fori_loop(0, chunks, finish_stores, 0)
+    lax.fori_loop(0, blocks, finish_stores, 0)
+
+
+def hand_on(*refs):
+    sources, targets, buffers, sems = refs[:3], refs[3:6], refs[6:9], refs[9]
+    parts = [(k, c) for k in range(2) for c in range(3)] + [(2, c) for c in range(4)]
+    moves = []
+    for n, (k, c) in enumerate(parts):
+        at = c if k < 2 else pl.ds(c * (sources[2].shape[0] // 4), sources[2].shape[0] // 4)
+        moves.append((
+            pltpu.make_async_copy(sources[k].at[at], buffers[k].at[at], sems.at[0, n]),
+            pltpu.make_async_copy(buffers[k].at[at], targets[k].at[at], sems.at[1, n]),
+        ))
+    for into, _ in moves:
+        into.start()
+    for into, out in moves:
+        into.wait()
+        out.start()
+    for _, out in moves:
+        out.wait()
 
 
 def shards(n_gx, n_gy, *args):
@@ -660,6 +737,7 @@
             pltpu.VMEM((zp, ROWS, 128), jnp.int32),
             vmem(zp, 8, 128),
             vmem(2, zp, 8, 128),
+            vmem(K, TILES, 2, 8, 128),
             vmem(2, nz + CH, 8, 128),
             vmem(2, nz + CH, 8, 128),
             vmem(2, chunks + 1, 8, 128),
@@ -678,17 +756,17 @@
             vmem(nz, 8, 128),
             vmem(nz, 8, 128),
             dma((6,)),
-            dma((3, chunks)),
-            dma((8, chunks)),
-            dma((2, 8, chunks)),
+            dma((3, nz // BLOCK)),
+            dma((8, nz // BLOCK)),
+            dma((2, 8, nz // BLOCK)),
             dma((n_gx,)),
             dma((n_gx,)),
             dma((2,)),
             dma((2,)),
             dma((2,)),
             dma((2,)),
-            dma((2,)),
-            dma((2,)),
+            dma((2, nz // BLOCK)),
+            dma((2, nz // BLOCK)),
         ],
         compiler_params=pltpu.CompilerParams(
             collective_id=0, has_side_effects=True, vmem_limit_bytes=56 << 20
@@ -699,7 +777,13 @@
         mode_profile.reshape(-1, mode_profile.shape[2]),
         sheet_offset, plane_start, monitor_length,
     )
-    return e, h, g * (1.0 / TICKS)
+    return pl.pallas_call(
+        hand_on,
+        out_shape=[jax.ShapeDtypeStruct(x.shape, f32) for x in (e, h, g)],
+        in_specs=[anyspace] * 3,
+        out_specs=[anyspace] * 3,
+        scratch_shapes=[vmem(*x.shape) for x in (e, h, g)] + [dma((2, 10))],
+    )(e, h, g)
 
 
 def solution(mesh):

time: 137 us -> 105 us (0.77)
  the two profiles are of different devices: /device:TPU:163 before, /device:TPU:44 now
where the time goes in v3:
time: 105 us
  Pallas kernels  102 us (97%)
  between operations  2.58 us (2%)
    pallas_call x1, Pallas kernels, shards(): pl.pallas_call(functools.partial(kernel, n_gx, n_gy, nz), out_shape=[jax....  98.9 us
    pallas_call x1, Pallas kernels, shards(): pl.pallas_call(hand_on, out_shape=[jax.ShapeDtypeStruct(x.shape, f32) for...  3.04 us

profile of v3, /device:TPU:44, one launch (start us, length us, event | category | flops | bytes accessed | tf_op | source)
XLA Modules:
  0.0 104.5 jit_solution(16922890676547514642)
XLA Ops:
  2.6 98.9 %shard_map.130 = (f32[3,32,32,128]{3,2,1,0:T(8,128)}, f32[3,32,32,128]{3,2,1,0:T(8,128)}, f32[32,32,128]{2,1,0:T(8,128)}) custom-call(f32[3,32,32,128]{3,2,1,0:T(8,128)} %e_in.1, f32[3,32,32,128]{3,2,1,0:T(8,128)} %h_in.1, f32[3,32,32,128]{3,2,1,0:T(8,128)} %f_in.1, s32[32,32,128]{2,1,0:T(8,128)} %material_in.1, f32[4]{0:T(128)} %inverse.1, ...), custom_call_target="tpu_custom_call" | custom-call | tf_op jit(solution)/shard_map/pallas_call | solution.py:721
  101.5 3.0 %shard_map.131 = (f32[3,32,32,128]{3,2,1,0:T(8,128)}, f32[3,32,32,128]{3,2,1,0:T(8,128)}, f32[32,32,128]{2,1,0:T(8,128)}) custom-call(f32[3,32,32,128]{3,2,1,0:T(8,128)} %get-tuple-element.6.refs_0_, f32[3,32,32,128]{3,2,1,0:T(8,128)} %get-tuple-element.7.refs_1_, f32[32,32,128]{2,1,0:T(8,128)} %get-tuple-element.8.refs_2_), custom_call_target="tpu_custom_call" | custom-call | tf_op jit(solution)/shard_map/pallas_call | solution.py:780

commit v4 on v3

--- a/solution.py
+++ b/solution.py
@@ -12,7 +12,7 @@
 K = 4
 ROUNDS = TICKS // K
 CH = 4
-BLOCK = 8
+BLOCK = 4
 TILES = 5
 TOP = 8
 ROWS = 56
@@ -649,7 +649,7 @@
 
             @pl.when(i == 1)
             def _():
-                done = n - 2
+                done = n - 3
                 done_r = (done + blocks) // blocks
                 done_q = lax.rem(done + blocks, blocks)
 

time: 105 us -> 103 us (0.981)
  the two profiles are of different devices: /device:TPU:44 before, /device:TPU:33 now
where the time goes in v4:
time: 103 us
  Pallas kernels  101 us (98%)
  between operations  2.58 us (3%)
    pallas_call x1, Pallas kernels, shards(): pl.pallas_call(functools.partial(kernel, n_gx, n_gy, nz), out_shape=[jax....  97.6 us
    pallas_call x1, Pallas kernels, shards(): pl.pallas_call(hand_on, out_shape=[jax.ShapeDtypeStruct(x.shape, f32) for...  3.04 us

profile of v4, /device:TPU:33, one launch (start us, length us, event | category | flops | bytes accessed | tf_op | source)
XLA Modules:
  0.0 103.2 jit_solution(13026548020190503029)
XLA Ops:
  2.6 97.6 %shard_map.130 = (f32[3,32,32,128]{3,2,1,0:T(8,128)}, f32[3,32,32,128]{3,2,1,0:T(8,128)}, f32[32,32,128]{2,1,0:T(8,128)}) custom-call(f32[3,32,32,128]{3,2,1,0:T(8,128)} %e_in.1, f32[3,32,32,128]{3,2,1,0:T(8,128)} %h_in.1, f32[3,32,32,128]{3,2,1,0:T(8,128)} %f_in.1, s32[32,32,128]{2,1,0:T(8,128)} %material_in.1, f32[4]{0:T(128)} %inverse.1, ...), custom_call_target="tpu_custom_call" | custom-call | tf_op jit(solution)/shard_map/pallas_call | solution.py:721
  100.2 3.0 %shard_map.131 = (f32[3,32,32,128]{3,2,1,0:T(8,128)}, f32[3,32,32,128]{3,2,1,0:T(8,128)}, f32[32,32,128]{2,1,0:T(8,128)}) custom-call(f32[3,32,32,128]{3,2,1,0:T(8,128)} %get-tuple-element.6.refs_0_, f32[3,32,32,128]{3,2,1,0:T(8,128)} %get-tuple-element.7.refs_1_, f32[32,32,128]{2,1,0:T(8,128)} %get-tuple-element.8.refs_2_), custom_call_target="tpu_custom_call" | custom-call | tf_op jit(solution)/shard_map/pallas_call | solution.py:780

commit v5 on v4

--- a/solution.py
+++ b/solution.py
@@ -747,7 +747,7 @@
             vmem(8, 128),
             vmem(n_gx, 8, 128),
             vmem(64, 40 * nz),
-            vmem(40 * nz, 128),
+            vmem(41 * nz, 128),
             pltpu.VMEM((zp, 48, 128), jnp.bfloat16),
             pltpu.VMEM((TICKS, 128, 256), jnp.bfloat16),
             vmem(2, nz, 8, 128),

time: 103 us -> 103 us (level)
  no operation moved by 1% of the time
where the time goes in v5:
time: 103 us
  Pallas kernels  101 us (98%)
  between operations  2.58 us (3%)
    pallas_call x1, Pallas kernels, shards(): pl.pallas_call(functools.partial(kernel, n_gx, n_gy, nz), out_shape=[jax....  97.6 us
    pallas_call x1, Pallas kernels, shards(): pl.pallas_call(hand_on, out_shape=[jax.ShapeDtypeStruct(x.shape, f32) for...  3.04 us

profile of v5, /device:TPU:33, one launch (start us, length us, event | category | flops | bytes accessed | tf_op | source)
XLA Modules:
  0.0 103.2 jit_solution(17238432665439679881)
XLA Ops:
  2.6 97.6 %shard_map.130 = (f32[3,32,32,128]{3,2,1,0:T(8,128)}, f32[3,32,32,128]{3,2,1,0:T(8,128)}, f32[32,32,128]{2,1,0:T(8,128)}) custom-call(f32[3,32,32,128]{3,2,1,0:T(8,128)} %e_in.1, f32[3,32,32,128]{3,2,1,0:T(8,128)} %h_in.1, f32[3,32,32,128]{3,2,1,0:T(8,128)} %f_in.1, s32[32,32,128]{2,1,0:T(8,128)} %material_in.1, f32[4]{0:T(128)} %inverse.1, ...), custom_call_target="tpu_custom_call" | custom-call | tf_op jit(solution)/shard_map/pallas_call | solution.py:721
  100.2 3.0 %shard_map.131 = (f32[3,32,32,128]{3,2,1,0:T(8,128)}, f32[3,32,32,128]{3,2,1,0:T(8,128)}, f32[32,32,128]{2,1,0:T(8,128)}) custom-call(f32[3,32,32,128]{3,2,1,0:T(8,128)} %get-tuple-element.6.refs_0_, f32[3,32,32,128]{3,2,1,0:T(8,128)} %get-tuple-element.7.refs_1_, f32[32,32,128]{2,1,0:T(8,128)} %get-tuple-element.8.refs_2_), custom_call_target="tpu_custom_call" | custom-call | tf_op jit(solution)/shard_map/pallas_call | solution.py:780
